TPU v7x, 32 devices: a whole 2x2x4 slice. The times are simulated.
32 devices in a mesh: grp: 2 (over y), ev: 4 (over z), src: 4 (over x, core).
Axes of the slice: x: 2, y: 2, z: 4, core: 2. Of those that a mesh axis runs over, the one named last changes fastest.
Arguments:
- sink_tensor: bfloat16 [4, 256, 256, 256], P('grp', 'ev'), parts along dimension 0, may hold values from -6 to 6
- source_tensor: bfloat16 [4, 2, 256, 256, 256], P('src', None, None, 'ev'), may hold values from -6 to 6
- perambulators: bfloat16 [8, 4, 2, 256, 256], P('src', None, None, 'ev'), may hold values from -0.25 to 0.25
- source_times: int32 [4], replicated, may hold values from 0 to 7, as said below
- spin_index: int32 [2, 3], replicated, may hold values from 0 to 3
Outputs:
- correlator: float32 [4, 4, 2], P('src', 'grp'), parts along dimension 1
There are 2 independent parts, one for each index of `grp`. A program takes and returns all parts, laid end to end along the dimension named above; an argument that names none is the same for every part. Nothing has to cross between parts.
Inputs may be any that keep to these rules, and one draw needn't show every extreme that they name: `source_times`: each contracted source time's perambulator time lies in a block of 2 consecutive times other than block i, where i is the contracted source time's own position.
All inputs are finite; a program needn't handle non-finite values.
Results may differ from a plain program's by a relative error of at most 0.0048.
Values may be sent and summed in bfloat16 or wider, within the bound.
No kernel may reach another device: no remote copies, remote signals or barrier semaphores. Data moves between devices by JAX's collectives and lax.ppermute only.
A program may use at most 256 MiB of HBM per device.

v0:
```python
import jax
import jax.numpy as jnp
from jax import lax
from jax.sharding import PartitionSpec as P


def apply_mode(tensor, matrix, pattern):
    first = jnp.einsum(pattern, tensor[0], matrix[0], preferred_element_type=jnp.float32)
    second = jnp.einsum(pattern, tensor[1], matrix[1], preferred_element_type=jnp.float32)
    third = jnp.einsum(pattern, tensor[0], matrix[1], preferred_element_type=jnp.float32)
    fourth = jnp.einsum(pattern, tensor[1], matrix[0], preferred_element_type=jnp.float32)
    return jnp.stack([first - second, third + fourth])


def inner_product(sink_side, source_side):
    real_part = jnp.sum(sink_side[0] * source_side[0] + sink_side[1] * source_side[1])
    imag_part = jnp.sum(sink_side[1] * source_side[0] - sink_side[0] * source_side[1])
    return jnp.stack([real_part, imag_part])


def project_two(sink_tensor, per_time, spin_row):
    second_map = lax.dynamic_index_in_dim(per_time, spin_row[1], 0, keepdims=False)
    third_map = lax.dynamic_index_in_dim(per_time, spin_row[2], 0, keepdims=False)
    after_last = apply_mode(sink_tensor, third_map, "abc,cd->abd").astype(jnp.bfloat16)
    return apply_mode(after_last, second_map, "abc,bd->adc").astype(jnp.bfloat16)


def finish(regrouped, per_time, spin_row, source_side, scale):
    first_map = lax.dynamic_index_in_dim(per_time, spin_row[0], 0, keepdims=False)
    sink_side = apply_mode(regrouped, first_map, "abc,ad->dbc")
    return inner_product(sink_side, source_side) * scale


def body(sink_tensor, source_tensor, perambulators, source_times, spin_index):
    position = lax.axis_index("src")
    own_time = lax.dynamic_index_in_dim(source_times, position, 0, keepdims=False)
    every_time = lax.all_gather(perambulators, "src", axis=0, tiled=True)
    own_block = lax.dynamic_index_in_dim(every_time, own_time, 0, keepdims=True)
    gathered = lax.all_gather(own_block, "ev", axis=3, tiled=True)
    per_time = gathered[0]
    structures = spin_index.shape[0]
    source_side = source_tensor[0]
    scale = float(sink_tensor.shape[3]) ** (-1.5)
    results = []
    for structure in range(structures):
        projected = project_two(sink_tensor, per_time, spin_index[structure])
        regrouped = lax.all_to_all(projected, "ev", split_axis=2, concat_axis=1, tiled=True)
        results.append(finish(regrouped, per_time, spin_index[structure], source_side, scale))
    partial_sums = jnp.stack(results)
    totals = lax.psum(partial_sums, "ev")
    return totals[None]


def solution(mesh):
    in_specs = (
        P("grp", "ev", None, None),
        P("src", None, None, "ev", None),
        P("src", None, None, "ev", None),
        P(),
        P(),
    )
    out_specs = P("src", "grp", None)
    return jax.shard_map(body, mesh=mesh, in_specs=in_specs, out_specs=out_specs, check_vma=False)
```

profile of v0, /device:TPU:0, one launch (start us, length us, event | category | flops | bytes accessed | tf_op | source)
XLA Modules:
  0.0 1051.9 jit_solution(12094448556931728950)
XLA Ops:
  10.5 23.7 %all-gather.3.cloned.1.call-done = bf16[8,4,2,64,256]{4,3,2,1,0:T(8,128)(2,1)} async-done(((bf16[2,4,2,64,256]{4,3,2,1,0:T(8,128)(2,1)}), bf16[8,4,2,64,256]{4,3,2,1,0:T(8,128)(2,1)}) %all-gather.3.cloned.1.call-update) | async-done | bytes 2097168 | tf_op jit(solution)/shard_map/all_gather | solution.py:37
  49.4 14.8 %all-gather.5.cloned.1.call-done = bf16[1,4,2,256,256]{4,1,2,0,3:T(4,128)(2,1)} async-done(((bf16[1,4,2,64,256]{4,1,2,0,3:T(4,128)(2,1)}), bf16[1,4,2,256,256]{4,1,2,0,3:T(4,128)(2,1)}) %all-gather.5.cloned.1.call-update) | async-done | bytes 1048592 | tf_op jit(solution)/shard_map/all_gather | solution.py:39
  83.2 11.6 %fusion.26 = f32[256,64,256]{2,0,1:T(8,128)} fusion(bf16[2,64,256,256]{3,2,1,0:T(8,128)(2,1)} %param.5, bf16[1,1,1,256,256]{3,4,2,1,0:T(8,128)(2,1)S(1)} %copy.66), kind=kOutput, calls=%fused_computation.52 | convolution fusion | flops 2147483648 | bytes 25296896 | tf_op jit(solution)/shard_map/abc,cd->abd/dot_general | solution.py:8
  94.8 13.5 %add_convert_fusion.1 = bf16[256,64,256]{2,0,1:T(8,128)(2,1)} fusion(f32[256,64,256]{2,0,1:T(8,128)} %fusion.24, bf16[2,64,256,256]{3,2,1,0:T(8,128)(2,1)} %param.5, bf16[1,1,1,256,256]{3,4,2,1,0:T(8,128)(2,1)S(1)} %copy.66), kind=kOutput, calls=%fused_computation.22 | convolution fusion | flops 2155872256 | bytes 33685504 | tf_op jit(solution)/shard_map/abc,cd->abd/dot_general | solution.py:11
  108.3 13.7 %subtract_convert_fusion.1 = bf16[256,64,256]{2,0,1:T(8,128)(2,1)} fusion(f32[256,64,256]{2,0,1:T(8,128)} %fusion.26, bf16[2,64,256,256]{3,2,1,0:T(8,128)(2,1)} %param.5, bf16[1,1,1,256,256]{3,4,2,1,0:T(8,128)(2,1)S(1)} %copy.67), kind=kOutput, calls=%fused_computation.23 | convolution fusion | flops 2155872256 | bytes 33685504 | tf_op jit(solution)/shard_map/abc,cd->abd/dot_general | solution.py:9
  122.0 11.7 %fusion.10 = f32[256,64,256]{2,0,1:T(8,128)} fusion(bf16[256,64,256]{2,0,1:T(8,128)(2,1)} %subtract_convert_fusion.1, bf16[1,1,1,256,256]{3,4,2,1,0:T(8,128)(2,1)S(1)} %copy.68), kind=kOutput, calls=%fused_computation.36 | convolution fusion | flops 2147483648 | bytes 25296896 | tf_op jit(solution)/shard_map/abc,bd->adc/dot_general | solution.py:10
  142.0 13.5 %fusion.49 = bf16[1,64,256,256]{3,2,1,0:T(8,128)(2,1)} fusion(f32[256,64,256]{2,0,1:T(8,128)} %fusion.10, bf16[256,64,256]{2,0,1:T(8,128)(2,1)} %add_convert_fusion.1, bf16[1,1,1,256,256]{3,4,2,1,0:T(8,128)(2,1)S(1)} %copy.64), kind=kOutput, calls=%fused_computation.69 | convolution fusion | flops 2155872256 | bytes 33685504 | tf_op jit(solution)/shard_map/abc,bd->adc/dot_general | solution.py:11
  155.5 13.5 %fusion.46 = bf16[1,64,256,256]{3,2,1,0:T(8,128)(2,1)} fusion(f32[256,64,256]{2,0,1:T(8,128)} %fusion.12, bf16[256,64,256]{2,0,1:T(8,128)(2,1)} %add_convert_fusion.1, bf16[1,1,1,256,256]{3,4,2,1,0:T(8,128)(2,1)S(1)} %copy.68), kind=kOutput, calls=%fused_computation.68 | convolution fusion | flops 2155872256 | bytes 33685504 | tf_op jit(solution)/shard_map/abc,bd->adc/dot_general | solution.py:9
  177.0 24.2 %copy.40 = bf16[2,64,256,256]{3,1,0,2:T(8,128)(2,1)} copy(bf16[2,64,256,256]{3,2,1,0:T(8,128)(2,1)S(1)} %pad_maximum_fusion.1) | data formatting | bytes 33554432 | tf_op jit(solution)/shard_map/stack | solution.py:12
  232.2 13.5 %subtract_convert_fusion.3 = bf16[256,64,256]{2,0,1:T(8,128)(2,1)} fusion(f32[256,64,256]{2,0,1:T(8,128)} %fusion.30, bf16[2,64,256,256]{3,2,1,0:T(8,128)(2,1)} %param.5, bf16[1,1,1,256,256]{3,4,2,1,0:T(8,128)(2,1)S(1)} %copy.56), kind=kOutput, calls=%fused_computation.27 | convolution fusion | flops 2155872256 | bytes 33685504 | tf_op jit(solution)/shard_map/abc,cd->abd/dot_general | solution.py:9
  245.8 11.6 %fusion.16 = f32[256,64,256]{2,0,1:T(8,128)} fusion(bf16[256,64,256]{2,0,1:T(8,128)(2,1)} %subtract_convert_fusion.3, bf16[1,1,1,256,256]{3,4,2,1,0:T(8,128)(2,1)S(1)} %copy.57), kind=kOutput, calls=%fused_computation.42 | convolution fusion | flops 2147483648 | bytes 25296896 | tf_op jit(solution)/shard_map/abc,bd->adc/dot_general | solution.py:10
  265.6 13.7 %add_convert_fusion.3 = bf16[256,64,256]{2,0,1:T(8,128)(2,1)} fusion(f32[256,64,256]{2,0,1:T(8,128)} %fusion.28, bf16[2,64,256,256]{3,2,1,0:T(8,128)(2,1)} %param.5, bf16[1,1,1,256,256]{3,4,2,1,0:T(8,128)(2,1)S(1)} %copy.55), kind=kOutput, calls=%fused_computation.26 | convolution fusion | flops 2155872256 | bytes 33685504 | tf_op jit(solution)/shard_map/abc,cd->abd/dot_general | solution.py:11
  279.3 13.5 %fusion.43 = bf16[1,64,256,256]{3,2,1,0:T(8,128)(2,1)} fusion(f32[256,64,256]{2,0,1:T(8,128)} %fusion.16, bf16[256,64,256]{2,0,1:T(8,128)(2,1)} %add_convert_fusion.3, bf16[1,1,1,256,256]{3,4,2,1,0:T(8,128)(2,1)S(1)} %copy.53), kind=kOutput, calls=%fused_computation.67 | convolution fusion | flops 2155872256 | bytes 33685504 | tf_op jit(solution)/shard_map/abc,bd->adc/dot_general | solution.py:11
  292.8 13.5 %fusion.40 = bf16[1,64,256,256]{3,2,1,0:T(8,128)(2,1)} fusion(f32[256,64,256]{2,0,1:T(8,128)} %fusion.18, bf16[256,64,256]{2,0,1:T(8,128)(2,1)} %add_convert_fusion.3, bf16[1,1,1,256,256]{3,4,2,1,0:T(8,128)(2,1)S(1)} %copy.57), kind=kOutput, calls=%fused_computation.66 | convolution fusion | flops 2155872256 | bytes 33685504 | tf_op jit(solution)/shard_map/abc,bd->adc/dot_general | solution.py:9
  314.4 24.2 %copy.29 = bf16[2,64,256,256]{3,1,0,2:T(8,128)(2,1)} copy(bf16[2,64,256,256]{3,2,1,0:T(8,128)(2,1)S(1)} %pad_maximum_fusion) | data formatting | bytes 33554432 | tf_op jit(solution)/shard_map/stack | solution.py:12
  338.6 233.0 %all-to-all-done.1 = bf16[2,64,256,256]{3,1,0,2:T(8,128)(2,1)} async-done(((bf16[2,64,256,256]{3,1,0,2:T(8,128)(2,1)}), bf16[2,64,256,256]{3,1,0,2:T(8,128)(2,1)}, u32[]{:S(2)}, u32[]{:S(2)}) %all-to-all-start.1) | async-done | bytes 16777248 | tf_op jit(solution)/shard_map/all_to_all | solution.py:47
  578.9 12.0 %fusion.81 = (bf16[1,1,256,64,256]{4,3,2,1,0:T(8,128)(2,1)}, bf16[1,1,256,64,256]{4,3,2,1,0:T(8,128)(2,1)}) fusion(bf16[1,2,256,64,256]{4,3,2,1,0:T(8,128)(2,1)} %param.6), kind=kLoop, calls=%fused_computation.115 | loop fusion | bytes 33554432 | tf_op jit(solution)/shard_map/slice | solution.py:16
  591.6 14.2 %copy.90 = bf16[2,64,4,64,256]{4,1,2,3,0:T(8,128)(2,1)} copy(bf16[2,64,4,64,256]{4,1,0,3,2:T(8,128)(2,1)} %bitcast.63) | data formatting | bytes 33554432 | tf_op jit(solution)/shard_map/all_to_all | solution.py:47
  628.8 13.9 %convolution_add_fusion = f32[256,64,256]{2,0,1:T(8,128)} fusion(f32[256,64,256]{2,0,1:T(8,128)} %fusion.55, bf16[256,64,256]{2,0,1:T(8,128)(2,1)S(1)} %bitcast.209, bf16[1,1,1,256,256]{3,4,2,1,0:T(8,128)(2,1)S(1)} %copy.62), kind=kOutput, calls=%fused_computation.28 | convolution fusion | flops 2151677952 | bytes 42074112 | tf_op jit(solution)/shard_map/abc,ad->dbc/dot_general | solution.py:11
  642.7 13.9 %convolution_subtract_fusion = f32[256,64,256]{2,0,1:T(8,128)} fusion(f32[256,64,256]{2,0,1:T(8,128)} %fusion.53, bf16[256,64,256]{2,0,1:T(8,128)(2,1)S(1)} %bitcast.210, bf16[1,1,1,256,256]{3,4,2,1,0:T(8,128)(2,1)S(1)} %copy.69), kind=kOutput, calls=%fused_computation.29 | convolution fusion | flops 2151677952 | bytes 42074112 | tf_op jit(solution)/shard_map/abc,ad->dbc/dot_general | solution.py:9
  656.6 284.7 %all-to-all-done = bf16[2,64,256,256]{3,1,0,2:T(8,128)(2,1)} async-done(((bf16[2,64,256,256]{3,1,0,2:T(8,128)(2,1)}), bf16[2,64,256,256]{3,1,0,2:T(8,128)(2,1)}, u32[]{:S(2)}, u32[]{:S(2)}) %all-to-all-start) | async-done | bytes 16777248 | tf_op jit(solution)/shard_map/all_to_all | solution.py:47
  941.2 14.1 %copy.91 = bf16[2,64,4,64,256]{4,1,2,3,0:T(8,128)(2,1)} copy(bf16[2,64,4,64,256]{4,1,0,3,2:T(8,128)(2,1)} %bitcast.26) | data formatting | bytes 33554432 | tf_op jit(solution)/shard_map/all_to_all | solution.py:47
  978.9 13.8 %convolution_add_fusion.1 = f32[256,64,256]{2,0,1:T(8,128)} fusion(f32[256,64,256]{2,0,1:T(8,128)} %fusion.69, bf16[256,64,256]{2,0,1:T(8,128)(2,1)S(1)} %bitcast.207, bf16[1,1,1,256,256]{3,4,2,1,0:T(8,128)(2,1)S(1)} %copy.51), kind=kOutput, calls=%fused_computation.30 | convolution fusion | flops 2151677952 | bytes 42074112 | tf_op jit(solution)/shard_map/abc,ad->dbc/dot_general | solution.py:11
  992.7 38.9 %fusion.1 = (f32[]{:T(128)}, f32[]{:T(128)}, f32[]{:T(128)}, f32[]{:T(128)}) fusion(f32[256,64,256]{2,0,1:T(8,128)} %convolution_add_fusion.1, bf16[1,1,256,64,256]{4,3,2,1,0:T(8,128)(2,1)} %get-tuple-element.14, bf16[1,1,256,64,256]{4,3,2,1,0:T(8,128)(2,1)} %get-tuple-element.13, f32[256,64,256]{2,0,1:T(8,128)} %convolution_subtract_fusion, ...), kind=kOutput, calls=%fused_computation.9 | convolution fusion | flops 2227175424 | bytes 92405776 | tf_op jit(solution)/shard_map/abc,ad->dbc/dot_general | solution.py:9
  (53 shorter events, 155.3 us)
Async XLA Ops:
  6.5 27.7 %all-gather.3.cloned.1.call-start = ((), (), s32[]{:S(2)}) async-start(), calls=%async_computation.2 | async-start | bytes 2621440 | tf_op jit(solution)/shard_map/all_gather | solution.py:37
  7.3 57.0 %all-gather.5.cloned.1.call-start = ((), (), s32[]{:S(2)}) async-start(), calls=%async_computation.3 | async-start | bytes 1310720 | tf_op jit(solution)/shard_map/all_gather | solution.py:39
  122.0 11.7 %copy-start.1 = (bf16[256,64,256]{2,0,1:T(8,128)(2,1)S(1)}, bf16[256,64,256]{2,0,1:T(8,128)(2,1)}, u32[]{:S(2)}) copy-start(bf16[256,64,256]{2,0,1:T(8,128)(2,1)} %subtract_convert_fusion.1) | copy-start | bytes 25165828
  201.2 370.4 %all-to-all-start.1 = ((bf16[2,64,256,256]{3,1,0,2:T(8,128)(2,1)}), bf16[2,64,256,256]{3,1,0,2:T(8,128)(2,1)}, u32[]{:S(2)}, u32[]{:S(2)}) async-start(bf16[2,64,256,256]{3,1,0,2:T(8,128)(2,1)} %copy.40), calls=%async_computation.1 | async-start | bytes 33554432 | tf_op jit(solution)/shard_map/all_to_all | solution.py:47
  245.8 11.6 %copy-start.2 = (bf16[256,64,256]{2,0,1:T(8,128)(2,1)S(1)}, bf16[256,64,256]{2,0,1:T(8,128)(2,1)}, u32[]{:S(2)}) copy-start(bf16[256,64,256]{2,0,1:T(8,128)(2,1)} %subtract_convert_fusion.3) | copy-start | bytes 25165828
  571.6 369.7 %all-to-all-start = ((bf16[2,64,256,256]{3,1,0,2:T(8,128)(2,1)}), bf16[2,64,256,256]{3,1,0,2:T(8,128)(2,1)}, u32[]{:S(2)}, u32[]{:S(2)}) async-start(bf16[2,64,256,256]{3,1,0,2:T(8,128)(2,1)} %copy.29), calls=%async_computation | async-start | bytes 33554432 | tf_op jit(solution)/shard_map/all_to_all | solution.py:47
  578.9 12.0 %copy-start.6 = (bf16[1,1,1,256,256]{4,1,2,0,3:T(2,128)(2,1)S(1)}, bf16[1,1,1,256,256]{4,1,2,0,3:T(2,128)(2,1)}, u32[]{:S(2)}) copy-start(bf16[1,1,1,256,256]{4,1,2,0,3:T(2,128)(2,1)} %get-tuple-element.17) | copy-start | bytes 393220
  578.9 12.2 %copy-start.5 = (bf16[1,1,1,256,256]{4,1,2,0,3:T(2,128)(2,1)S(1)}, bf16[1,1,1,256,256]{4,1,2,0,3:T(2,128)(2,1)}, u32[]{:S(2)}) copy-start(bf16[1,1,1,256,256]{4,1,2,0,3:T(2,128)(2,1)} %get-tuple-element.20) | copy-start | bytes 393220
  578.9 12.3 %copy-start.4 = (bf16[1,1,1,256,256]{4,1,2,0,3:T(2,128)(2,1)S(1)}, bf16[1,1,1,256,256]{4,1,2,0,3:T(2,128)(2,1)}, u32[]{:S(2)}) copy-start(bf16[1,1,1,256,256]{4,1,2,0,3:T(2,128)(2,1)} %get-tuple-element.23) | copy-start | bytes 393220
  578.9 12.5 %copy-start.3 = (bf16[1,1,1,256,256]{4,1,2,0,3:T(2,128)(2,1)S(1)}, bf16[1,1,1,256,256]{4,1,2,0,3:T(2,128)(2,1)}, u32[]{:S(2)}) copy-start(bf16[1,1,1,256,256]{4,1,2,0,3:T(2,128)(2,1)} %get-tuple-element.27) | copy-start | bytes 393220
  962.5 16.4 %copy-start = (bf16[1,4,64,64,256]{4,2,1,3,0:T(8,128)(2,1)}, bf16[1,4,64,64,256]{4,2,1,3,0:T(8,128)(2,1)S(1)}, u32[]{:S(2)}) copy-start(bf16[1,4,64,64,256]{4,2,1,3,0:T(8,128)(2,1)S(1)} %get-tuple-element.15) | copy-start | bytes 25165828
Sparse Core Ops, SparseCore 0:
  8.9 25.2 all-gather.2
  36.3 27.9 all-gather.4
where the time goes:
time: 1060 us; the launch traced here: 1050 us
  waiting for transfers between devices  557 us (53%)
  matrix products  308 us (29%)
  local copies, waits for them, and re-layouts  116 us (11%)
  between operations  27.7 us (3%)
  other arithmetic  18.6 us (2%)
  starting transfers between devices  14.8 us (1%)
    all_to_all x2, waiting for transfers between devices, body(): lax.all_to_all(projected, 'ev', split_axis=2, concat_axis=1, tiled=True)  518 us
    dot_general x6, matrix products, apply_mode(): jnp.einsum(pattern, tensor[1], matrix[1], preferred_element_type=jnp.floa...  107 us
    dot_general x6, matrix products, apply_mode(): jnp.einsum(pattern, tensor[1], matrix[0], preferred_element_type=jnp.floa...  82 us
    dot_general x6, matrix products, apply_mode(): jnp.einsum(pattern, tensor[0], matrix[1], preferred_element_type=jnp.floa...  62.8 us
    dot_general x6, matrix products, apply_mode(): jnp.einsum(pattern, tensor[0], matrix[0], preferred_element_type=jnp.floa...  55.8 us
    another operation x2, local copies, waits for them, and re-layouts, apply_mode(): return jnp.stack([first - second, third + fourth])  48.4 us
    all_to_all x2, local copies, waits for them, and re-layouts, body(): lax.all_to_all(projected, 'ev', split_axis=2, concat_axis=1, tiled=True)  28.3 us
    all_gather x1, waiting for transfers between devices, body(): every_time = lax.all_gather(perambulators, 'src', axis=0, tiled=True)  23.7 us
  transfers between devices with their start and end apart: 4, of which 4 were waited for; matrix products, arithmetic and copies ran while one was open for 20% of the time, Pallas kernels for 0%

commit v1 on v0

v1 whole, which is shorter than its diff:
```python
import functools

import jax
import jax.numpy as jnp
from jax import lax
from jax.experimental import pallas as pl
from jax.experimental.pallas import tpu as pltpu
from jax.sharding import PartitionSpec as P

BF16, F32 = jnp.bfloat16, jnp.float32
LANES = 128
BLOCK = 8


def project_kernel(left_ref, source_ref, out_ref):
    structures, _, halves, _, rows, lanes = out_ref.shape
    for i in range(source_ref.shape[0]):
        got = jnp.dot(left_ref[...], source_ref[i], preferred_element_type=F32)
        for h in range(halves):
            out_ref[:, :, h, i] = got[:, h * lanes : (h + 1) * lanes].reshape(structures, 2, rows, lanes)


def project_source(left, source, structures):
    e, k, n = source.shape
    rows = left.shape[0] // (2 * structures)
    halves = n // LANES
    per = 4
    return pl.pallas_call(
        project_kernel,
        grid=(e // per,),
        in_specs=[
            pl.BlockSpec(left.shape, lambda i: (0, 0)),
            pl.BlockSpec((per, k, n), lambda i: (i, 0, 0)),
        ],
        out_specs=pl.BlockSpec((structures, 2, halves, per, rows, LANES), lambda i: (0, 0, 0, i, 0, 0)),
        out_shape=jax.ShapeDtypeStruct((structures, 2, halves, e, rows, LANES), F32),
        compiler_params=pltpu.CompilerParams(vmem_limit_bytes=48 * 1024 * 1024),
        cost_estimate=pl.CostEstimate(
            flops=2 * left.shape[0] * k * n * e,
            bytes_accessed=2 * source.size + 4 * left.shape[0] * e * n,
            transcendentals=0,
        ),
        name="project_source",
    )(left, source)


def contract_kernel(at_ref, sink_ref, *refs, sources):
    t_refs, (q_ref, w_ref, acc_ref, out_ref) = refs[:sources], refs[sources:]
    _, block, n, _ = sink_ref.shape
    structures, _, halves, e, _, lanes = t_refs[0].shape

    @pl.when(pl.program_id(0) == 0)
    def _():
        out_ref[...] = acc_ref[...]

    @pl.when(at_ref[2] > 0)
    def _():
        re_rows = sink_ref[0].reshape(block * n, n)
        im_rows = sink_ref[1].reshape(block * n, n)
        for g in range(sources):
            t_rows = t_refs[g].reshape(structures * 2 * halves * e * block, lanes)
            for s in range(structures):
                c = g * structures + s
                acc = [[jnp.zeros((8, lanes), F32) for _ in range(halves)] for _ in range(2)]
                first = jnp.dot(re_rows, w_ref[c, 0], preferred_element_type=F32)
                first += jnp.dot(im_rows, w_ref[c, 1], preferred_element_type=F32)
                first = first.astype(BF16)
                for a in range(block):
                    one = first[a * n : (a + 1) * n]
                    second = jnp.dot(q_ref[c, 0], one[:, :n], preferred_element_type=F32)
                    second += jnp.dot(q_ref[c, 1], one[:, n:], preferred_element_type=F32)
                    second = second.astype(BF16).astype(F32)
                    for h in range(halves):
                        re = second[:e, h * lanes : (h + 1) * lanes]
                        im = second[e:, h * lanes : (h + 1) * lanes]
                        base = (s * 2 * halves + h) * e * block + a
                        tre = t_rows[pl.ds(base, e, stride=block), :]
                        tim = t_rows[pl.ds(base + halves * e * block, e, stride=block), :]
                        acc[0][h] += (re * tre - im * tim).reshape(e // 8, 8, lanes).sum(0)
                        acc[1][h] += (re * tim + im * tre).reshape(e // 8, 8, lanes).sum(0)
                for part in range(2):
                    for h in range(halves):
                        out_ref[c, part, h] += acc[part][h]


def contract(sink, sink_block, ts, t_block, valid, q, w, acc, blocks):
    n = sink.shape[2]
    structures, _, halves, e, _, lanes = ts[0].shape
    whole = lambda ref: pl.BlockSpec(ref.shape, lambda i, at: (0,) * ref.ndim)
    at = jnp.stack([jnp.asarray(v, jnp.int32) for v in (sink_block, t_block, valid)])
    combos = w.shape[0]
    return pl.pallas_call(
        functools.partial(contract_kernel, sources=len(ts)),
        grid_spec=pltpu.PrefetchScalarGridSpec(
            num_scalar_prefetch=1,
            grid=(blocks,),
            in_specs=[pl.BlockSpec((2, BLOCK, n, n), lambda i, at: (0, at[0] + i, 0, 0))]
            + [pl.BlockSpec((structures, 2, halves, e, BLOCK, lanes), lambda i, at: (0, 0, 0, 0, at[1] + i, 0))] * len(ts)
            + [whole(q), whole(w), whole(acc)],
            out_specs=whole(acc),
        ),
        out_shape=jax.ShapeDtypeStruct(acc.shape, F32),
        compiler_params=pltpu.CompilerParams(vmem_limit_bytes=56 * 1024 * 1024),
        cost_estimate=pl.CostEstimate(
            flops=blocks * BLOCK * combos * 2 * (n * 2 * n * 2 * n + 2 * e * 2 * n * n),
            bytes_accessed=blocks * BLOCK * (4 * n * n + combos * 8 * e * n),
            transcendentals=0,
        ),
        name="contract",
    )(at, sink, *ts, q, w, acc)


def own_maps(perambulators, source_times):
    position, srcs = lax.axis_index("src"), lax.axis_size("src")
    held = perambulators.shape[0]
    own_time = lax.dynamic_index_in_dim(source_times, position, 0, keepdims=False)
    chosen = None
    for k in range(1, srcs):
        to = lax.rem(position + srcs - k, srcs)
        within = lax.dynamic_index_in_dim(source_times, to, 0, keepdims=False) - position * held
        within = jnp.clip(within, 0, held - 1)
        sent = lax.dynamic_index_in_dim(perambulators, within, 0, keepdims=False)
        got = lax.ppermute(sent, "src", [(j, (j + srcs - k) % srcs) for j in range(srcs)])
        here = own_time // held == lax.rem(position + k, srcs)
        chosen = got if chosen is None else jnp.where(here, got, chosen)
    return lax.all_gather(chosen, "ev", axis=2, tiled=True)


def pick(per_time, spin):
    return lax.dynamic_index_in_dim(per_time, spin, 0, keepdims=False)


def left_of(per_time, spin_index, rows):
    out = []
    for s in range(spin_index.shape[0]):
        p = rows(pick(per_time, spin_index[s, 0]))
        out += [jnp.concatenate([p[0], p[1]], 1), jnp.concatenate([p[1], -p[0]], 1)]
    return jnp.concatenate(out, 0)


def middle_of(per_time, spin_index, ev, e):
    out = []
    for s in range(spin_index.shape[0]):
        p = pick(per_time, spin_index[s, 1])
        p = lax.dynamic_slice_in_dim(p, ev * e, e, axis=2).transpose(0, 2, 1)
        out.append(jnp.stack([jnp.concatenate([p[0], p[1]], 0), jnp.concatenate([-p[1], p[0]], 0)]))
    return jnp.stack(out)


def right_of(per_time, spin_index):
    out = []
    for s in range(spin_index.shape[0]):
        p = pick(per_time, spin_index[s, 2])
        out.append(jnp.stack([jnp.concatenate([p[0], p[1]], 1), jnp.concatenate([-p[1], p[0]], 1)]))
    return jnp.stack(out)


def body_any(sink_tensor, source_tensor, perambulators, source_times, spin_index):
    position, ev = lax.axis_index("src"), lax.axis_index("ev")
    evs, srcs = lax.axis_size("ev"), lax.axis_size("src")
    structures = spin_index.shape[0]
    _, slice_a, n, _ = sink_tensor.shape
    e = n // evs
    share = slice_a // srcs
    mine = lax.dynamic_slice_in_dim(sink_tensor, position * share, share, axis=1)
    sink = lax.all_gather(mine, ("ev", "src"), axis=1, tiled=True)
    per_time = own_maps(perambulators, source_times)
    source = source_tensor[0].reshape(2 * n, e, n).transpose(1, 0, 2)
    t = project_source(left_of(per_time, spin_index, lambda p: p), source, structures)
    q, w = middle_of(per_time, spin_index, ev, e), right_of(per_time, spin_index)
    acc = jnp.zeros((structures, 2, n // LANES, 8, LANES), F32)
    acc = contract(sink, 0, [t], 0, 1, q, w, acc, n // BLOCK)
    return lax.psum(acc.sum((2, 3, 4)), "ev")


def body_relay(sink_tensor, source_tensor, perambulators, source_times, spin_index):
    position, ev, grp = lax.axis_index("src"), lax.axis_index("ev"), lax.axis_index("grp")
    evs, srcs = lax.axis_size("ev"), lax.axis_size("src")
    structures = spin_index.shape[0]
    _, slice_a, n, _ = sink_tensor.shape
    e = n // evs
    chip, core = position // 2, position % 2
    half = slice_a // 2
    units = half // BLOCK
    is_end = (ev == 0) | (ev == evs - 1)
    is_inner = jnp.logical_not(is_end)
    near = jnp.where(ev < 2, 1 - ev, 5 - ev)
    opposite = 3 - ev
    across = 3 - near

    def unit(w):
        return jnp.where(chip == 0, w, units - 1 - w)

    def partner_unit(w):
        return jnp.where(chip == 0, units - 1 - w, w)

    def own(w):
        return lax.dynamic_slice_in_dim(sink_tensor, core * half + BLOCK * unit(w), BLOCK, axis=1)

    both = lambda v: lax.ppermute(v, "ev", [(0, 1), (1, 0), (2, 3), (3, 2)])
    outward = lambda v: lax.ppermute(v, "ev", [(1, 0), (2, 3)])
    inward = lambda v: lax.ppermute(v, "ev", [(0, 1), (3, 2)])
    middle = lambda v: lax.ppermute(v, "ev", [(1, 2), (2, 1)])
    swap_chips = lambda v: lax.ppermute(v, "src", [(0, 2), (2, 0), (1, 3), (3, 1)])
    swap_cores = lambda v: lax.ppermute(v, "src", [(0, 1), (1, 0), (2, 3), (3, 2)])
    swap_groups = lambda v: lax.ppermute(v, "grp", [(0, 1), (1, 0)])

    own0, own1, own2 = own(0), own(1), own(2)
    a1, b1 = both(own0), middle(own0)
    per_time = own_maps(perambulators, source_times)
    source = source_tensor[0].reshape(2 * n, e, n).transpose(1, 0, 2)
    other_source = swap_cores(source)
    other_time = swap_cores(per_time)

    rows = lambda p: lax.dynamic_index_in_dim(p.reshape(2, evs, 2, half, n), core, 2, keepdims=False).reshape(2, n // 2, n)
    times = (per_time, other_time)
    ts = [
        project_source(left_of(p, spin_index, rows), src, structures)
        for p, src in zip(times, (source, other_source))
    ]
    q = jnp.concatenate([middle_of(p, spin_index, ev, e) for p in times])
    q_near = jnp.concatenate([middle_of(p, spin_index, near, e) for p in times])
    w = jnp.concatenate([right_of(p, spin_index) for p in times])
    acc = jnp.zeros((2 * structures, 2, n // LANES, 8, LANES), F32)

    x1 = swap_chips(a1)
    b2 = middle(a1)
    a2 = both(jnp.where(is_end, own1, b1))
    x2 = swap_chips(jnp.where(is_end, a2, b1))
    b3 = middle(own1)
    a3 = both(jnp.where(is_end, own2, b2))
    x3 = swap_chips(jnp.where(is_end, a3, b2))
    b4 = middle(a2)
    a4 = outward(b3)
    x4 = swap_chips(jnp.where(is_end, a4, b3))
    a5 = outward(b4)
    x5 = swap_chips(jnp.where(is_end, a5, b4))
    block = near * units + 1 + grp
    sent = jnp.stack([lax.dynamic_slice_in_dim(t, block * BLOCK, BLOCK, axis=4) for t in ts]).astype(BF16)
    near_t = inward(sent)
    far_t = swap_groups(near_t)

    def add(acc, unit_array, end_slice, inner_slice, end_unit, inner_unit, valid=1):
        t_block = jnp.where(is_end, end_slice * units + end_unit, inner_slice * units + inner_unit)
        return contract(unit_array, 0, ts, t_block, valid, q, w, acc, 1)

    acc = contract(sink_tensor, core * units, ts, ev * units, 1, q, w, acc, units)
    acc = add(acc, a1, near, near, unit(0), unit(0))
    acc = add(acc, b1, 0, opposite, 0, unit(0), is_inner)
    acc = add(acc, a2, across, near, unit(0), unit(1))
    acc = add(acc, b2, 0, across, 0, unit(0), is_inner)
    acc = add(acc, x1, near, near, partner_unit(0), partner_unit(0))
    acc = add(acc, a3, opposite, near, unit(0), unit(2))
    acc = add(acc, b3, 0, opposite, 0, unit(1), is_inner)
    acc = add(acc, x2, across, opposite, partner_unit(0), partner_unit(0))
    acc = add(acc, a4, across, 0, unit(1), 0, is_end)
    acc = add(acc, b4, 0, across, 0, unit(1), is_inner)
    acc = add(acc, x3, opposite, across, partner_unit(0), partner_unit(0))
    for received, which in ((near_t, grp), (far_t, 1 - grp)):
        wide = [received[g].astype(F32) for g in range(2)]
        acc = contract(sink_tensor, core * units + 1 + which, wide, 0, is_inner, q_near, w, acc, 1)
    acc = add(acc, a5, opposite, 0, unit(1), 0, is_end)
    acc = add(acc, x4, across, opposite, partner_unit(1), partner_unit(1))
    acc = add(acc, x5, opposite, across, partner_unit(1), partner_unit(1))

    part = acc.sum((2, 3, 4)).reshape(2, structures, 2)
    each = jnp.arange(srcs)[:, None, None]
    placed = jnp.where(each == position, part[0], 0.0) + jnp.where(each == position + 1 - 2 * core, part[1], 0.0)
    return lax.psum(placed, ("ev", "src"))[position]


def body(relay, *args):
    totals = (body_relay if relay else body_any)(*args)
    return (totals * float(args[0].shape[3]) ** -1.5)[None]


def solution(mesh):
    relay = mesh.shape["ev"] == 4 and mesh.shape["src"] == 4 and mesh.shape["grp"] == 2
    in_specs = (
        P("grp", "ev", None, None),
        P("src", None, None, "ev", None),
        P("src", None, None, "ev", None),
        P(),
        P(),
    )
    out_specs = P("src", "grp", None)
    return jax.shard_map(functools.partial(body, relay), mesh=mesh, in_specs=in_specs, out_specs=out_specs, check_vma=False)
```

time: 1060 us -> 638 us (0.60)
  waiting for transfers between devices: 557 us -> 169 us
  matrix products: 308 us -> 0 us
  Pallas kernels: 0 us -> 225 us
  local copies, waits for them, and re-layouts: 116 us -> 38.3 us
  starting transfers between devices: 14.8 us -> 82.1 us
  blocking collectives: 10.4 us -> 38.7 us
  other arithmetic: 18.6 us -> 45.3 us
    all_to_all x2 -> x0, waiting for transfers between devices: 518 us -> none  [body(): lax.all_to_all(projected, 'ev', split_axis=2, concat_axis=1, tiled=True)]
    dot_general x24 -> x0, matrix products: 308 us -> none  [the longest x6 107 us: apply_mode(): jnp.einsum(pattern, tensor[1], matrix[1], preferred_element_type=jnp.floa...]
    pallas_call x0 -> x19, Pallas kernels: none -> 225 us  [the longest x17 177 us: contract(): pl.pallas_call(functools.partial(contract_kernel, sources=len(ts)), grid_...]
    ppermute x0 -> x21, waiting for transfers between devices: none -> 143 us  [the longest x2 81.5 us: body_relay(): outward = lambda v: lax.ppermute(v, 'ev', [(1, 0), (2, 3)])]
    ppermute x0 -> x21, starting transfers between devices: none -> 82.1 us  [the longest x3 60.7 us: body_relay(): both = lambda v: lax.ppermute(v, 'ev', [(0, 1), (1, 0), (2, 3), (3, 2)])]
    another operation x2, local copies, waits for them, and re-layouts: 48.4 us -> 3.51 us  [body_relay(): jnp.stack([lax.dynamic_slice_in_dim(t, block * BLOCK, BLOCK, axis=4) for...]
    slice x5 -> x4, local copies, waits for them, and re-layouts: 34.3 us -> 0.67 us  [the longest x1 0.61 us: right_of(): p = pick(per_time, spin_index[s, 2])]
    psum x1, blocking collectives: 10.4 us -> 38.7 us  [body_relay(): return lax.psum(placed, ('ev', 'src'))[position]]
  transfers between devices with their start and end apart: 4 -> 22, of which waited for: 4 -> 7; matrix products, arithmetic and copies ran while one was open for 20% -> 10% of each run, Pallas kernels for 0% -> 34%
where the time goes in v1:
time: 638 us; the launch traced here: 628 us
  Pallas kernels  225 us (35%)
  waiting for transfers between devices  169 us (26%)
  starting transfers between devices  82.1 us (13%)
  other arithmetic  45.3 us (7%)
  blocking collectives  38.7 us (6%)
  local copies, waits for them, and re-layouts  38.3 us (6%)
  between operations  30.1 us (5%)
    pallas_call x17, Pallas kernels, contract(): pl.pallas_call(functools.partial(contract_kernel, sources=len(ts)), grid_...  177 us
    ppermute x2, waiting for transfers between devices, body_relay(): outward = lambda v: lax.ppermute(v, 'ev', [(1, 0), (2, 3)])  81.5 us
    ppermute x3, starting transfers between devices, body_relay(): both = lambda v: lax.ppermute(v, 'ev', [(0, 1), (1, 0), (2, 3), (3, 2)])  60.7 us
    pallas_call x2, Pallas kernels, project_source(): pl.pallas_call(project_kernel, grid=(e // per,), in_specs=[pl.BlockSpec(l...  47.5 us
    ppermute x3, waiting for transfers between devices, body_relay(): both = lambda v: lax.ppermute(v, 'ev', [(0, 1), (1, 0), (2, 3), (3, 2)])  46.9 us
    psum x1, blocking collectives, body_relay(): return lax.psum(placed, ('ev', 'src'))[position]  38.7 us
    all_gather x1, waiting for transfers between devices, own_maps(): return lax.all_gather(chosen, 'ev', axis=2, tiled=True)  25.6 us
    unnamed x49, local copies, waits for them, and re-layouts  18.1 us
  transfers between devices with their start and end apart: 22, of which 7 were waited for; matrix products, arithmetic and copies ran while one was open for 10% of the time, Pallas kernels for 34%

profile of v1, /device:TPU:0, one launch (start us, length us, event | category | flops | bytes accessed | tf_op | source)
XLA Modules:
  0.0 628.1 jit_solution(12170718565233204930)
XLA Ops:
  6.5 15.7 %copy.7 = bf16[1,2,256,64,256]{4,2,1,3,0:T(8,128)(2,1)} copy(bf16[1,2,256,64,256]{4,3,2,1,0:T(8,128)(2,1)} %param.6) | data formatting | bytes 33554432 | tf_op args[1]
  39.3 8.5 %collective-permute-done.5 = bf16[4,2,64,256]{3,2,1,0:T(8,128)(2,1)S(1)} collective-permute-done((bf16[4,2,64,256]{3,2,1,0:T(8,128)(2,1)S(1)}, bf16[4,2,64,256]{3,2,1,0:T(8,128)(2,1)S(1)}, u32[]{:S(2)}, u32[]{:S(2)}) %collective-permute-start.5) | collective-permute-done | bytes 262176 | tf_op jit(solution)/shard_map/ppermute | solution.py:123
  68.8 25.6 %all-gather.2.cloned.1.call-done = bf16[4,2,256,256]{3,2,1,0:T(8,128)(2,1)} async-done(((bf16[4,2,64,256]{3,2,1,0:T(8,128)(2,1)}), bf16[4,2,256,256]{3,2,1,0:T(8,128)(2,1)}) %all-gather.2.cloned.1.call-update) | async-done | bytes 1048592 | tf_op jit(solution)/shard_map/all_gather | solution.py:126
  106.8 6.7 %broadcast_select_fusion.4 = (bf16[2,8,256,256]{3,2,1,0:T(8,128)(2,1)}, bf16[2,8,256,256]{3,2,1,0:T(8,128)(2,1)}, bf16[2,8,256,256]{3,2,1,0:T(8,128)(2,1)}) fusion(bf16[2,8,256,256]{3,2,1,0:T(8,128)(2,1)S(1)} %collective-permute-done.sink_ref, pred[]{:T(512)S(6)} %or.3, bf16[2,64,256,256]{3,2,1,0:T(8,128)(2,1)} %sink_ref.5, s32[]{:T(128)S(6)} %select_n.235, ...), kind=kLoop, calls=%fused_computation.9 | loop fusion | flops 2097152 | bytes 14680073 | tf_op jit(solution)/shard_map/jit(_where)/select_n | solution.py:228
  113.5 54.7 %collective-permute-start.1 = (bf16[2,8,256,256]{3,2,1,0:T(8,128)(2,1)}, bf16[2,8,256,256]{3,2,1,0:T(8,128)(2,1)}, u32[]{:S(2)}, u32[]{:S(2)}) collective-permute-start(bf16[2,8,256,256]{3,2,1,0:T(8,128)(2,1)} %get-tuple-element.13), channel_id=1, source_target_pairs={{0,4},{4,0},{8,12},{12,8},{1,5},{5,1},{9,13},{13,9},{2,6},{6,2},{1... | collective-permute-start | bytes 6291464 | tf_op jit(solution)/shard_map/ppermute | solution.py:200
  168.2 23.8 %project_source.2.refs_0_ = f32[2,2,2,64,128,128]{5,4,3,2,1,0:T(8,128)} custom-call(bf16[512,512]{1,0:T(8,128)(2,1)S(1)} %maximum_maximum_fusion.left_ref, bf16[64,512,256]{2,1,0:T(8,128)(2,1)} %bitcast.17.source_ref), custom_call_target="tpu_custom_call" | custom-call | flops 8589934592 | bytes 50331648 | tf_op jit(solution)/shard_map/project_source/pallas_call | solution.py:28
  204.0 9.9 %collective-permute-done.1.sink_ref = bf16[2,8,256,256]{3,2,1,0:T(8,128)(2,1)} collective-permute-done((bf16[2,8,256,256]{3,2,1,0:T(8,128)(2,1)}, bf16[2,8,256,256]{3,2,1,0:T(8,128)(2,1)}, u32[]{:S(2)}, u32[]{:S(2)}) %collective-permute-start.1) | collective-permute-done | bytes 2097184 | tf_op jit(solution)/shard_map/ppermute | solution.py:200
  230.3 37.0 %collective-permute-done.17.sink_ref = bf16[2,8,256,256]{3,2,1,0:T(8,128)(2,1)S(1)} collective-permute-done((bf16[2,8,256,256]{3,2,1,0:T(8,128)(2,1)S(1)}, bf16[2,8,256,256]{3,2,1,0:T(8,128)(2,1)S(1)}, u32[]{:S(2)}, u32[]{:S(2)}) %collective-permute-start.17) | collective-permute-done | bytes 2097184 | tf_op jit(solution)/shard_map/ppermute | solution.py:200
  270.3 41.9 %collective-permute-done.11.sink_ref = bf16[2,8,256,256]{3,2,1,0:T(8,128)(2,1)S(1)} collective-permute-done((bf16[2,8,256,256]{3,2,1,0:T(8,128)(2,1)S(1)}, bf16[2,8,256,256]{3,2,1,0:T(8,128)(2,1)S(1)}, u32[]{:S(2)}, u32[]{:S(2)}) %collective-permute-start.11) | collective-permute-done | bytes 2097184 | tf_op jit(solution)/shard_map/ppermute | solution.py:201
  315.3 39.5 %collective-permute-done.3.sink_ref = bf16[2,8,256,256]{3,2,1,0:T(8,128)(2,1)S(1)} collective-permute-done((bf16[2,8,256,256]{3,2,1,0:T(8,128)(2,1)S(1)}, bf16[2,8,256,256]{3,2,1,0:T(8,128)(2,1)S(1)}, u32[]{:S(2)}, u32[]{:S(2)}) %collective-permute-start.3) | collective-permute-done | bytes 2097184 | tf_op jit(solution)/shard_map/ppermute | solution.py:201
  357.8 23.7 %project_source.3.refs_1_ = f32[2,2,2,64,128,128]{5,4,3,2,1,0:T(8,128)} custom-call(bf16[512,512]{1,0:T(8,128)(2,1)S(1)} %maximum_maximum_fusion.1.left_ref, bf16[64,512,256]{2,1,0:T(8,128)(2,1)} %collective-permute-done.9.source_ref), custom_call_target="tpu_custom_call" | custom-call | flops 8589934592 | bytes 50331648 | tf_op jit(solution)/shard_map/project_source/pallas_call | solution.py:28
  388.4 31.1 %contract.17.refs_4_ = f32[4,2,2,8,128]{4,3,2,1,0:T(8,128)} custom-call(s32[3]{0:T(128)} %pad_add_fusion.14.at_ref, bf16[2,64,256,256]{3,2,1,0:T(8,128)(2,1)} %sink_ref.5, f32[2,2,2,64,128,128]{5,4,3,2,1,0:T(8,128)} %project_source.2.refs_0_, f32[2,2,2,64,128,128]{5,4,3,2,1,0:T(8,128)} %project_source.3.refs_1_, ...), custom_call_target="tpu_custom_call" | custom-call | flops 21474836480 | bytes 25165824 | tf_op jit(solution)/shard_map/contract/pallas_call | solution.py:92
  419.5 11.5 %contract.18.refs_4_ = f32[4,2,2,8,128]{4,3,2,1,0:T(8,128)} custom-call(s32[3]{0:T(128)} %pad_add_fusion.15.at_ref, bf16[2,8,256,256]{3,2,1,0:T(8,128)(2,1)} %collective-permute-done.15.sink_ref, f32[2,2,2,64,128,128]{5,4,3,2,1,0:T(8,128)} %project_source.2.refs_0_, f32[2,2,2,64,128,128]{5,4,3,2,1,0:T(8,128)} %project_source.3.refs_1_, ...), custom_call_target="tpu_custom_call" | custom-call | flops 5368709120 | bytes 6291456 | tf_op jit(solution)/shard_map/contract/pallas_call | solution.py:92
  436.1 11.5 %contract.20.refs_4_ = f32[4,2,2,8,128]{4,3,2,1,0:T(8,128)} custom-call(s32[3]{0:T(128)} %get-tuple-element.103.at_ref, bf16[2,8,256,256]{3,2,1,0:T(8,128)(2,1)} %collective-permute-done.1.sink_ref, f32[2,2,2,64,128,128]{5,4,3,2,1,0:T(8,128)} %project_source.2.refs_0_, f32[2,2,2,64,128,128]{5,4,3,2,1,0:T(8,128)} %project_source.3.refs_1_, ...), custom_call_target="tpu_custom_call" | custom-call | flops 5368709120 | bytes 6291456 | tf_op jit(solution)/shard_map/contract/pallas_call | solution.py:92
  453.5 11.5 %contract.22.refs_4_ = f32[4,2,2,8,128]{4,3,2,1,0:T(8,128)} custom-call(s32[3]{0:T(128)} %pad_add_fusion.17.at_ref, bf16[2,8,256,256]{3,2,1,0:T(8,128)(2,1)} %collective-permute-done.20.sink_ref, f32[2,2,2,64,128,128]{5,4,3,2,1,0:T(8,128)} %project_source.2.refs_0_, f32[2,2,2,64,128,128]{5,4,3,2,1,0:T(8,128)} %project_source.3.refs_1_, ...), custom_call_target="tpu_custom_call" | custom-call | flops 5368709120 | bytes 6291456 | tf_op jit(solution)/shard_map/contract/pallas_call | solution.py:92
  465.0 11.6 %contract.23.refs_4_ = f32[4,2,2,8,128]{4,3,2,1,0:T(8,128)} custom-call(s32[3]{0:T(128)} %pad_add_fusion.18.at_ref, bf16[2,8,256,256]{3,2,1,0:T(8,128)(2,1)} %copy-done.7, f32[2,2,2,64,128,128]{5,4,3,2,1,0:T(8,128)} %project_source.2.refs_0_, f32[2,2,2,64,128,128]{5,4,3,2,1,0:T(8,128)} %project_source.3.refs_1_, ...), custom_call_target="tpu_custom_call" | custom-call | flops 5368709120 | bytes 6291456 | tf_op jit(solution)/shard_map/contract/pallas_call | solution.py:92
  481.5 11.6 %contract.25.refs_4_ = f32[4,2,2,8,128]{4,3,2,1,0:T(8,128)} custom-call(s32[3]{0:T(128)} %pad_add_fusion.19.at_ref, bf16[2,8,256,256]{3,2,1,0:T(8,128)(2,1)} %collective-permute-done.19.sink_ref, f32[2,2,2,64,128,128]{5,4,3,2,1,0:T(8,128)} %project_source.2.refs_0_, f32[2,2,2,64,128,128]{5,4,3,2,1,0:T(8,128)} %project_source.3.refs_1_, ...), custom_call_target="tpu_custom_call" | custom-call | flops 5368709120 | bytes 6291456 | tf_op jit(solution)/shard_map/contract/pallas_call | solution.py:92
  494.7 11.4 %contract.26.refs_4_ = f32[4,2,2,8,128]{4,3,2,1,0:T(8,128)} custom-call(s32[3]{0:T(128)} %fusion.11.at_ref, bf16[2,8,256,256]{3,2,1,0:T(8,128)(2,1)} %copy-done.6, f32[2,2,2,64,128,128]{5,4,3,2,1,0:T(8,128)} %project_source.2.refs_0_, f32[2,2,2,64,128,128]{5,4,3,2,1,0:T(8,128)} %project_source.3.refs_1_, bf16[4,2,128,256]{3,2,1,0:T(8,128)(2,1)} %pad_maximum_fusion.2.refs_2_, ...), custom_call_target="tpu_custom_call" | custom-call | flops 5368709120 | bytes 6291456 | tf_op jit(solution)/shard_map/contract/pallas_call | solution.py:92
  511.4 11.5 %contract.28.refs_4_ = f32[4,2,2,8,128]{4,3,2,1,0:T(8,128)} custom-call(s32[3]{0:T(128)} %pad_add_fusion.20.at_ref, bf16[2,8,256,256]{3,2,1,0:T(8,128)(2,1)} %collective-permute-done.18.sink_ref, f32[2,2,2,64,128,128]{5,4,3,2,1,0:T(8,128)} %project_source.2.refs_0_, f32[2,2,2,64,128,128]{5,4,3,2,1,0:T(8,128)} %project_source.3.refs_1_, ...), custom_call_target="tpu_custom_call" | custom-call | flops 5368709120 | bytes 6291456 | tf_op jit(solution)/shard_map/contract/pallas_call | solution.py:92
  531.9 6.3 %collective-permute-done.14 = bf16[2,2,2,2,64,8,128]{6,5,4,3,2,1,0:T(8,128)(2,1)S(1)} collective-permute-done((bf16[2,2,2,2,64,8,128]{6,5,4,3,2,1,0:T(8,128)(2,1)}, bf16[2,2,2,2,64,8,128]{6,5,4,3,2,1,0:T(8,128)(2,1)S(1)}, u32[]{:S(2)}, u32[]{:S(2)}) %collective-permute-start.14) | collective-permute-done | bytes 2097184 | tf_op jit(solution)/shard_map/ppermute | solution.py:206
  545.6 11.6 %contract.31.refs_4_ = f32[4,2,2,8,128]{4,3,2,1,0:T(8,128)} custom-call(s32[3]{0:T(128)} %fusion.9.at_ref, bf16[2,8,256,256]{3,2,1,0:T(8,128)(2,1)} %copy-done.5, f32[2,2,2,64,128,128]{5,4,3,2,1,0:T(8,128)} %project_source.2.refs_0_, f32[2,2,2,64,128,128]{5,4,3,2,1,0:T(8,128)} %project_source.3.refs_1_, bf16[4,2,128,256]{3,2,1,0:T(8,128)(2,1)} %pad_maximum_fusion.2.refs_2_, ...), custom_call_target="tpu_custom_call" | custom-call | flops 5368709120 | bytes 6291456 | tf_op jit(solution)/shard_map/contract/pallas_call | solution.py:92
  557.2 11.4 %contract.32.refs_4_ = f32[4,2,2,8,128]{4,3,2,1,0:T(8,128)} custom-call(s32[3]{0:T(128)} %pad_add_fusion.21.at_ref, bf16[2,8,256,256]{3,2,1,0:T(8,128)(2,1)} %collective-permute-done.12.sink_ref, f32[2,2,2,64,128,128]{5,4,3,2,1,0:T(8,128)} %project_source.2.refs_0_, f32[2,2,2,64,128,128]{5,4,3,2,1,0:T(8,128)} %project_source.3.refs_1_, ...), custom_call_target="tpu_custom_call" | custom-call | flops 5368709120 | bytes 6291456 | tf_op jit(solution)/shard_map/contract/pallas_call | solution.py:92
  568.7 11.8 %contract.33 = f32[4,2,2,8,128]{4,3,2,1,0:T(8,128)} custom-call(s32[3]{0:T(128)} %pad_add_fusion.22.at_ref, bf16[2,8,256,256]{3,2,1,0:T(8,128)(2,1)} %collective-permute-done.4.sink_ref, f32[2,2,2,64,128,128]{5,4,3,2,1,0:T(8,128)} %project_source.2.refs_0_, f32[2,2,2,64,128,128]{5,4,3,2,1,0:T(8,128)} %project_source.3.refs_1_, ...), custom_call_target="tpu_custom_call" | custom-call | flops 5368709120 | bytes 6291456 | tf_op jit(solution)/shard_map/contract/pallas_call | solution.py:92
  581.5 38.7 %psum.7 = f32[4,2,2]{2,1,0:T(2,128)S(1)} all-reduce(f32[4,2,2]{2,1,0:T(2,128)S(1)} %select_add_fusion), channel_id=1, replica_groups=mesh['grp'=2,'ev'=4,'src'=4] {'ev','src'}, use_global_device_ids=true, to_apply=%region_1.2 | all-reduce | flops 16 | bytes 128 | tf_op jit(solution)/shard_map/psum | solution.py:269
  (188 shorter events, 119.4 us)
Async XLA Ops:
  6.5 87.9 %all-gather.2.cloned.1.call-start = ((), (), s32[]{:S(2)}) async-start(), calls=%async_computation | async-start | bytes 1310720 | tf_op jit(solution)/shard_map/all_gather | solution.py:126
  22.2 335.6 %collective-permute-start.9 = (bf16[64,512,256]{2,1,0:T(8,128)(2,1)}, bf16[64,512,256]{2,1,0:T(8,128)(2,1)}, u32[]{:S(2)}, u32[]{:S(2)}) collective-permute-start(bf16[64,512,256]{2,1,0:T(8,128)(2,1)} %bitcast.17.source_ref), channel_id=1, source_target_pairs={{0,1},{1,0},{2,3},{3,2},{4,5},{5,4},{6,7},{7,6},{8,9},{9,8},{10,11... | collective-permute-start | bytes 50331656 | tf_op jit(solution)/shard_map/ppermute | solution.py:205
  25.3 22.5 %collective-permute-start.5 = (bf16[4,2,64,256]{3,2,1,0:T(8,128)(2,1)S(1)}, bf16[4,2,64,256]{3,2,1,0:T(8,128)(2,1)S(1)}, u32[]{:S(2)}, u32[]{:S(2)}) collective-permute-start(bf16[4,2,64,256]{3,2,1,0:T(8,128)(2,1)S(1)} %get-tuple-element.41), channel_id=1, source_target_pairs={{0,1},{1,2},{2,3},{3,0},{4,5},{5,6},{6,7},{7,4},{8,9},{9,10},{10,1... | collective-permute-start | bytes 786440 | tf_op jit(solution)/shard_map/ppermute | solution.py:123
  25.5 23.2 %collective-permute-start.6 = (bf16[4,2,64,256]{3,2,1,0:T(8,128)(2,1)S(1)}, bf16[4,2,64,256]{3,2,1,0:T(8,128)(2,1)S(1)}, u32[]{:S(2)}, u32[]{:S(2)}) collective-permute-start(bf16[4,2,64,256]{3,2,1,0:T(8,128)(2,1)S(1)} %get-tuple-element.42), channel_id=1, source_target_pairs={{0,2},{1,3},{2,0},{3,1},{4,6},{5,7},{6,4},{7,5},{8,10},{9,11},{10,... | collective-permute-start | bytes 786440 | tf_op jit(solution)/shard_map/ppermute | solution.py:123
  28.4 20.3 %collective-permute-start.7 = (bf16[4,2,64,256]{3,2,1,0:T(8,128)(2,1)S(1)}, bf16[4,2,64,256]{3,2,1,0:T(8,128)(2,1)S(1)}, u32[]{:S(2)}, u32[]{:S(2)}) collective-permute-start(bf16[4,2,64,256]{3,2,1,0:T(8,128)(2,1)S(1)} %get-tuple-element.40), channel_id=1, source_target_pairs={{0,3},{1,0},{2,1},{3,2},{4,7},{5,4},{6,5},{7,6},{8,11},{9,8},{10,9... | collective-permute-start | bytes 786440 | tf_op jit(solution)/shard_map/ppermute | solution.py:123
  32.4 69.9 %collective-permute-start.15 = (bf16[2,8,256,256]{3,2,1,0:T(8,128)(2,1)}, bf16[2,8,256,256]{3,2,1,0:T(8,128)(2,1)}, u32[]{:S(2)}, u32[]{:S(2)}) collective-permute-start(bf16[2,8,256,256]{3,2,1,0:T(8,128)(2,1)} %constant_dynamic-slice_fusion.21), channel_id=1, source_target_pairs={{0,4},{4,0},{8,12},{12,8},{1,5},{5,1},{9,13},{13,9},{2,6},{6,2},{1... | collective-permute-start | bytes 6291464 | tf_op jit(solution)/shard_map/ppermute | solution.py:200
  47.9 58.9 %collective-permute-start = (bf16[2,8,256,256]{3,2,1,0:T(8,128)(2,1)}, bf16[2,8,256,256]{3,2,1,0:T(8,128)(2,1)S(1)}, u32[]{:S(2)}, u32[]{:S(2)}) collective-permute-start(bf16[2,8,256,256]{3,2,1,0:T(8,128)(2,1)} %constant_dynamic-slice_fusion.21), channel_id=1, source_target_pairs={{4,8},{8,4},{5,9},{9,5},{6,10},{10,6},{7,11},{11,7},{20,24},{24,20... | collective-permute-start | bytes 6291464 | tf_op jit(solution)/shard_map/ppermute | solution.py:203
  99.1 96.2 %collective-permute-start.8 = (bf16[4,2,256,256]{3,2,1,0:T(8,128)(2,1)}, bf16[4,2,256,256]{3,2,1,0:T(8,128)(2,1)S(1)}, u32[]{:S(2)}, u32[]{:S(2)}) collective-permute-start(bf16[4,2,256,256]{3,2,1,0:T(8,128)(2,1)} %all-gather.2.cloned.1.call-done), channel_id=1, source_target_pairs={{0,1},{1,0},{2,3},{3,2},{4,5},{5,4},{6,7},{7,6},{8,9},{9,8},{10,11... | collective-permute-start | bytes 3145736 | tf_op jit(solution)/shard_map/ppermute | solution.py:205
  102.4 4.4 collective-permute-start.16
  106.7 120.3 %copy-start = (bf16[2,8,256,256]{3,2,1,0:T(8,128)(2,1)}, bf16[2,8,256,256]{3,2,1,0:T(8,128)(2,1)S(1)}, u32[]{:S(2)}) copy-start(bf16[2,8,256,256]{3,2,1,0:T(8,128)(2,1)S(1)} %collective-permute-done.sink_ref) | copy-start | bytes 6291460
  113.5 100.4 %collective-permute-start.1 = (bf16[2,8,256,256]{3,2,1,0:T(8,128)(2,1)}, bf16[2,8,256,256]{3,2,1,0:T(8,128)(2,1)}, u32[]{:S(2)}, u32[]{:S(2)}) collective-permute-start(bf16[2,8,256,256]{3,2,1,0:T(8,128)(2,1)} %get-tuple-element.13), channel_id=1, source_target_pairs={{0,4},{4,0},{8,12},{12,8},{1,5},{5,1},{9,13},{13,9},{2,6},{6,2},{1... | collective-permute-start | bytes 6291464 | tf_op jit(solution)/shard_map/ppermute | solution.py:200
  193.7 259.2 %collective-permute-start.20 = (bf16[2,8,256,256]{3,2,1,0:T(8,128)(2,1)}, bf16[2,8,256,256]{3,2,1,0:T(8,128)(2,1)}, u32[]{:S(2)}, u32[]{:S(2)}) collective-permute-start(bf16[2,8,256,256]{3,2,1,0:T(8,128)(2,1)} %collective-permute-done.15.sink_ref), channel_id=1, source_target_pairs={{0,2},{2,0},{1,3},{3,1},{4,6},{6,4},{5,7},{7,5},{8,10},{10,8},{9,1... | collective-permute-start | bytes 6291464 | tf_op jit(solution)/shard_map/ppermute | solution.py:204
  203.1 17.7 %collective-permute-start.10 = (bf16[2,8,256,256]{3,2,1,0:T(8,128)(2,1)}, bf16[2,8,256,256]{3,2,1,0:T(8,128)(2,1)S(1)}, u32[]{:S(2)}, u32[]{:S(2)}) collective-permute-start(bf16[2,8,256,256]{3,2,1,0:T(8,128)(2,1)} %get-tuple-element.14), channel_id=1, source_target_pairs={{4,8},{8,4},{5,9},{9,5},{6,10},{10,6},{7,11},{11,7},{20,24},{24,20... | collective-permute-start | bytes 6291464 | tf_op jit(solution)/shard_map/ppermute | solution.py:203
  213.9 9.3 %collective-permute-start.2 = (bf16[2,8,256,256]{3,2,1,0:T(8,128)(2,1)}, bf16[2,8,256,256]{3,2,1,0:T(8,128)(2,1)S(1)}, u32[]{:S(2)}, u32[]{:S(2)}) collective-permute-start(bf16[2,8,256,256]{3,2,1,0:T(8,128)(2,1)} %collective-permute-done.1.sink_ref), channel_id=1, source_target_pairs={{4,8},{8,4},{5,9},{9,5},{6,10},{10,6},{7,11},{11,7},{20,24},{24,20... | collective-permute-start | bytes 6291464 | tf_op jit(solution)/shard_map/ppermute | solution.py:203
  216.3 51.0 %collective-permute-start.17 = (bf16[2,8,256,256]{3,2,1,0:T(8,128)(2,1)S(1)}, bf16[2,8,256,256]{3,2,1,0:T(8,128)(2,1)S(1)}, u32[]{:S(2)}, u32[]{:S(2)}) collective-permute-start(bf16[2,8,256,256]{3,2,1,0:T(8,128)(2,1)S(1)} %copy-done.11), channel_id=1, source_target_pairs={{0,4},{4,0},{8,12},{12,8},{1,5},{5,1},{9,13},{13,9},{2,6},{6,2},{1... | collective-permute-start | bytes 6291464 | tf_op jit(solution)/shard_map/ppermute | solution.py:200
  220.8 91.4 %collective-permute-start.11 = (bf16[2,8,256,256]{3,2,1,0:T(8,128)(2,1)S(1)}, bf16[2,8,256,256]{3,2,1,0:T(8,128)(2,1)S(1)}, u32[]{:S(2)}, u32[]{:S(2)}) collective-permute-start(bf16[2,8,256,256]{3,2,1,0:T(8,128)(2,1)S(1)} %collective-permute-done.10.sink_ref), channel_id=1, source_target_pairs={{4,0},{8,12},{5,1},{9,13},{6,2},{10,14},{7,3},{11,15},{20,16},{24,... | collective-permute-start | bytes 6291464 | tf_op jit(solution)/shard_map/ppermute | solution.py:201
  223.1 133.2 %copy-start.3 = (bf16[2,8,256,256]{3,2,1,0:T(8,128)(2,1)}, bf16[2,8,256,256]{3,2,1,0:T(8,128)(2,1)S(1)}, u32[]{:S(2)}) copy-start(bf16[2,8,256,256]{3,2,1,0:T(8,128)(2,1)S(1)} %collective-permute-done.2.sink_ref) | copy-start | bytes 6291460
  223.1 131.7 %collective-permute-start.3 = (bf16[2,8,256,256]{3,2,1,0:T(8,128)(2,1)S(1)}, bf16[2,8,256,256]{3,2,1,0:T(8,128)(2,1)S(1)}, u32[]{:S(2)}, u32[]{:S(2)}) collective-permute-start(bf16[2,8,256,256]{3,2,1,0:T(8,128)(2,1)S(1)} %collective-permute-done.2.sink_ref), channel_id=1, source_target_pairs={{4,0},{8,12},{5,1},{9,13},{6,2},{10,14},{7,3},{11,15},{20,16},{24,... | collective-permute-start | bytes 6291464 | tf_op jit(solution)/shard_map/ppermute | solution.py:201
  267.3 214.2 %collective-permute-start.19 = (bf16[2,8,256,256]{3,2,1,0:T(8,128)(2,1)}, bf16[2,8,256,256]{3,2,1,0:T(8,128)(2,1)}, u32[]{:S(2)}, u32[]{:S(2)}) collective-permute-start(bf16[2,8,256,256]{3,2,1,0:T(8,128)(2,1)} %broadcast_select_fusion), channel_id=1, source_target_pairs={{0,2},{2,0},{1,3},{3,1},{4,6},{6,4},{5,7},{7,5},{8,10},{10,8},{9,1... | collective-permute-start | bytes 6291464 | tf_op jit(solution)/shard_map/ppermute | solution.py:204
  312.3 199.2 %collective-permute-start.18 = (bf16[2,8,256,256]{3,2,1,0:T(8,128)(2,1)}, bf16[2,8,256,256]{3,2,1,0:T(8,128)(2,1)}, u32[]{:S(2)}, u32[]{:S(2)}) collective-permute-start(bf16[2,8,256,256]{3,2,1,0:T(8,128)(2,1)} %broadcast_select_fusion.1), channel_id=1, source_target_pairs={{0,2},{2,0},{1,3},{3,1},{4,6},{6,4},{5,7},{7,5},{8,10},{10,8},{9,1... | collective-permute-start | bytes 6291464 | tf_op jit(solution)/shard_map/ppermute | solution.py:204
  354.8 202.4 %collective-permute-start.12 = (bf16[2,8,256,256]{3,2,1,0:T(8,128)(2,1)}, bf16[2,8,256,256]{3,2,1,0:T(8,128)(2,1)}, u32[]{:S(2)}, u32[]{:S(2)}) collective-permute-start(bf16[2,8,256,256]{3,2,1,0:T(8,128)(2,1)} %broadcast_select_fusion.2), channel_id=1, source_target_pairs={{0,2},{2,0},{1,3},{3,1},{4,6},{6,4},{5,7},{7,5},{8,10},{10,8},{9,1... | collective-permute-start | bytes 6291464 | tf_op jit(solution)/shard_map/ppermute | solution.py:204
  384.8 108.3 %collective-permute-start.13 = (bf16[2,2,2,2,64,8,128]{6,5,4,3,2,1,0:T(8,128)(2,1)}, bf16[2,2,2,2,64,8,128]{6,5,4,3,2,1,0:T(8,128)(2,1)}, u32[]{:S(2)}, u32[]{:S(2)}) collective-permute-start(bf16[2,2,2,2,64,8,128]{6,5,4,3,2,1,0:T(8,128)(2,1)} %pad_maximum_fusion.1), channel_id=1, source_target_pairs={{0,4},{12,8},{1,5},{13,9},{2,6},{14,10},{3,7},{15,11},{16,20},{28,... | collective-permute-start | bytes 6291464 | tf_op jit(solution)/shard_map/ppermute | solution.py:202
  452.9 115.8 %collective-permute-start.4 = (bf16[2,8,256,256]{3,2,1,0:T(8,128)(2,1)}, bf16[2,8,256,256]{3,2,1,0:T(8,128)(2,1)}, u32[]{:S(2)}, u32[]{:S(2)}) collective-permute-start(bf16[2,8,256,256]{3,2,1,0:T(8,128)(2,1)} %broadcast_select_fusion.3), channel_id=1, source_target_pairs={{0,2},{2,0},{1,3},{3,1},{4,6},{6,4},{5,7},{7,5},{8,10},{10,8},{9,1... | collective-permute-start | bytes 6291464 | tf_op jit(solution)/shard_map/ppermute | solution.py:204
  493.1 45.1 %collective-permute-start.14 = (bf16[2,2,2,2,64,8,128]{6,5,4,3,2,1,0:T(8,128)(2,1)}, bf16[2,2,2,2,64,8,128]{6,5,4,3,2,1,0:T(8,128)(2,1)S(1)}, u32[]{:S(2)}, u32[]{:S(2)}) collective-permute-start(bf16[2,2,2,2,64,8,128]{6,5,4,3,2,1,0:T(8,128)(2,1)} %collective-permute-done.13), channel_id=1, source_target_pairs={{0,16},{16,0},{1,17},{17,1},{2,18},{18,2},{3,19},{19,3},{4,20},{20... | collective-permute-start | bytes 6291464 | tf_op jit(solution)/shard_map/ppermute | solution.py:206
  (22 other events, 309.5 us)
Sparse Core Ops, SparseCore 0:
  49.6 44.8 all-gather.1

commit v2 on v0

v2 whole, which is shorter than its diff:
```python
import functools

import jax
import jax.numpy as jnp
import numpy as np
from jax import lax
from jax.experimental import pallas as pl
from jax.experimental.pallas import tpu as pltpu
from jax.sharding import PartitionSpec as P

BF16, F32 = jnp.bfloat16, jnp.float32
LANES = 128
BLOCK = 8


def project_kernel(left_ref, source_ref, out_ref, wide_ref):
    structures, _, halves, per, rows, lanes = out_ref.shape
    parts, n = source_ref.shape[:2]
    for part in range(parts):
        for h in range(halves):
            one = source_ref[part, :, :, h * lanes : (h + 1) * lanes]
            wide_ref[part, h] = one.astype(F32).reshape(n * per, lanes)
    for i in range(per):
        one = [
            jnp.concatenate([wide_ref[part, h, pl.ds(i, n, stride=per), :].astype(BF16) for h in range(halves)], 1)
            for part in range(parts)
        ]
        got = jnp.dot(left_ref[...], jnp.concatenate(one, 0), preferred_element_type=F32)
        for h in range(halves):
            out_ref[:, :, h, i] = got[:, h * lanes : (h + 1) * lanes].reshape(structures, 2, rows, lanes)


def project_source(left, source, structures):
    parts, _, e, n = source.shape
    rows = left.shape[0] // (2 * structures)
    halves = n // LANES
    per = min(16, e)
    return pl.pallas_call(
        project_kernel,
        grid=(e // per,),
        in_specs=[
            pl.BlockSpec(left.shape, lambda i: (0, 0)),
            pl.BlockSpec((parts, n, per, n), lambda i: (0, 0, i, 0)),
        ],
        out_specs=pl.BlockSpec((structures, 2, halves, per, rows, LANES), lambda i: (0, 0, 0, i, 0, 0)),
        out_shape=jax.ShapeDtypeStruct((structures, 2, halves, e, rows, LANES), F32),
        scratch_shapes=[pltpu.VMEM((parts, halves, n * per, LANES), F32)],
        compiler_params=pltpu.CompilerParams(vmem_limit_bytes=56 * 1024 * 1024),
        cost_estimate=pl.CostEstimate(
            flops=2 * left.shape[0] * 2 * n * n * e,
            bytes_accessed=2 * source.size + 4 * left.shape[0] * e * n,
            transcendentals=0,
        ),
        name="project_source",
    )(left, source)


def contract_block(sink, t_views, q_ref, w_ref, out_ref, e):
    _, block, n, _ = sink.shape
    combos, _, halves, _, lanes = out_ref.shape
    structures = combos // len(t_views)
    re_rows = sink[0].reshape(block * n, n)
    im_rows = sink[1].reshape(block * n, n)
    for g, t_rows in enumerate(t_views):
        for s in range(structures):
            c = g * structures + s
            acc = [[jnp.zeros((8, lanes), F32) for _ in range(halves)] for _ in range(2)]
            first = jnp.dot(re_rows, w_ref[c, 0], preferred_element_type=F32)
            first += jnp.dot(im_rows, w_ref[c, 1], preferred_element_type=F32)
            first = first.astype(BF16)
            for a in range(block):
                one = first[a * n : (a + 1) * n]
                second = jnp.dot(q_ref[c, 0], one[:, :n], preferred_element_type=F32)
                second += jnp.dot(q_ref[c, 1], one[:, n:], preferred_element_type=F32)
                second = second.astype(BF16).astype(F32)
                for h in range(halves):
                    re = second[:e, h * lanes : (h + 1) * lanes]
                    im = second[e:, h * lanes : (h + 1) * lanes]
                    base = (s * 2 * halves + h) * e * block + a
                    tre = t_rows[pl.ds(base, e, stride=block), :]
                    tim = t_rows[pl.ds(base + halves * e * block, e, stride=block), :]
                    acc[0][h] += (re * tre - im * tim).reshape(e // 8, 8, lanes).sum(0)
                    acc[1][h] += (re * tim + im * tre).reshape(e // 8, 8, lanes).sum(0)
            for part in range(2):
                for h in range(halves):
                    out_ref[c, part, h] += acc[part][h]


def t_view(ref):
    structures, _, halves, e, block, lanes = ref.shape
    return ref.reshape(structures * 2 * halves * e * block, lanes)


def contract_kernel(at_ref, sink_ref, *refs, sources, base):
    t_refs, (q_ref, w_ref, acc_ref, out_ref) = refs[:sources], refs[sources:]
    e = t_refs[0].shape[3]

    @pl.when(pl.program_id(0) == 0)
    def _():
        out_ref[...] = acc_ref[...]

    @pl.when(at_ref[base + 2] > 0)
    def _():
        contract_block(sink_ref, [t_view(t) for t in t_refs], q_ref, w_ref, out_ref, e)


def whole(ref):
    return pl.BlockSpec(ref.shape, lambda i, at: (0,) * ref.ndim)


def t_specs(ts, block_at):
    structures, _, halves, e, _, lanes = ts[0].shape
    shape = (structures, 2, halves, e, BLOCK, lanes)
    return [pl.BlockSpec(shape, lambda i, at: (0, 0, 0, 0, block_at(i, at), 0))] * len(ts)


def contract_cost(blocks, combos, n, e):
    return pl.CostEstimate(
        flops=blocks * BLOCK * combos * 2 * (n * 2 * n * 2 * n + 2 * e * 2 * n * n),
        bytes_accessed=blocks * BLOCK * (4 * n * n + combos * 8 * e * n),
        transcendentals=0,
    )


def scalars(*values):
    return jnp.stack([jnp.asarray(v, jnp.int32) for v in values])


def contract(sink, ts, table, base, q, w, acc, blocks):
    n = sink.shape[2]
    return pl.pallas_call(
        functools.partial(contract_kernel, sources=len(ts), base=base),
        grid_spec=pltpu.PrefetchScalarGridSpec(
            num_scalar_prefetch=1,
            grid=(blocks,),
            in_specs=[pl.BlockSpec((2, BLOCK, n, n), lambda i, at: (0, at[base] + i, 0, 0))]
            + t_specs(ts, lambda i, at: at[base + 1] + i)
            + [whole(q), whole(w), whole(acc)],
            out_specs=whole(acc),
        ),
        out_shape=jax.ShapeDtypeStruct(acc.shape, F32),
        compiler_params=pltpu.CompilerParams(vmem_limit_bytes=56 * 1024 * 1024),
        cost_estimate=contract_cost(blocks, w.shape[0], n, ts[0].shape[3]),
        name="contract",
    )(table, sink, *ts, q, w, acc)


def slots_kernel(at_ref, *refs, sources, shapes, base):
    arrays = sum(len(parts) for choices in shapes for parts in choices)
    sinks, refs = refs[:arrays], refs[arrays:]
    t_refs, (q_ref, w_ref, acc_ref, out_ref, held, sem) = refs[:sources], refs[sources:]
    e = t_refs[0].shape[3]
    i = pl.program_id(0)

    def fetch(slot):
        place = sum(len(parts) for choices in shapes[:slot] for parts in choices)
        for k, parts in enumerate(shapes[slot]):

            @pl.when(at_ref[base + 2 * slot] == k + 1)
            def _():
                row = 0
                for part, size in enumerate(parts):
                    to = held.at[slot % 2, :, pl.ds(row, size)]
                    pltpu.make_async_copy(sinks[place + part], to, sem.at[slot % 2]).start()
                    row += size

            place += len(parts)

    @pl.when(i == 0)
    def _():
        fetch(0)
        out_ref[...] = acc_ref[...]

    for slot in range(1, len(shapes)):

        @pl.when(i == slot - 1)
        def _():
            fetch(slot)

    @pl.when(at_ref[base + 2 * i] > 0)
    def _():
        now = lax.rem(i, 2)
        pltpu.make_async_copy(held.at[now], held.at[now], sem.at[now]).wait()
        contract_block(held.at[now], [t_view(t) for t in t_refs], q_ref, w_ref, out_ref, e)


def contract_slots(slots, ts, table, base, q, w, acc):
    n = q.shape[-1]
    arrays = [part for choices in slots for parts in choices for part in parts]
    shapes = tuple(tuple(tuple(part.shape[1] for part in parts) for parts in choices) for choices in slots)
    return pl.pallas_call(
        functools.partial(slots_kernel, sources=len(ts), shapes=shapes, base=base),
        grid_spec=pltpu.PrefetchScalarGridSpec(
            num_scalar_prefetch=1,
            grid=(len(slots),),
            in_specs=[pl.BlockSpec(memory_space=pl.ANY)] * len(arrays)
            + t_specs(ts, lambda i, at: at[base + 2 * i + 1])
            + [whole(q), whole(w), whole(acc)],
            out_specs=whole(acc),
            scratch_shapes=[pltpu.VMEM((2, 2, BLOCK, n, n), BF16), pltpu.SemaphoreType.DMA((2,))],
        ),
        out_shape=jax.ShapeDtypeStruct(acc.shape, F32),
        compiler_params=pltpu.CompilerParams(vmem_limit_bytes=56 * 1024 * 1024),
        cost_estimate=contract_cost(len(slots), w.shape[0], n, ts[0].shape[3]),
        name="contract_slots",
    )(table, *arrays, *ts, q, w, acc)


def near_kernel(at_ref, sink_ref, t_ref, q_ref, w_ref, acc_ref, out_ref, wide_ref, *, base):
    out_ref[...] = acc_ref[...]
    e = q_ref.shape[2] // 2

    @pl.when(at_ref[base + 1] > 0)
    def _():
        sources = t_ref.shape[0]
        wide_ref[...] = t_ref[...].reshape(wide_ref.shape).astype(F32)
        rows = wide_ref.shape[1]
        contract_block(sink_ref, [wide_ref.at[g] for g in range(sources)], q_ref, w_ref, out_ref, e)


def contract_near(sink, t, table, base, q, w, acc):
    n = sink.shape[2]
    return pl.pallas_call(
        functools.partial(near_kernel, base=base),
        grid_spec=pltpu.PrefetchScalarGridSpec(
            num_scalar_prefetch=1,
            grid=(1,),
            in_specs=[pl.BlockSpec((2, BLOCK, n, n), lambda i, at: (0, at[base], 0, 0)), whole(t), whole(q), whole(w), whole(acc)],
            out_specs=whole(acc),
            scratch_shapes=[pltpu.VMEM((t.shape[0], t.size // t.shape[0] // LANES, LANES), F32)],
        ),
        out_shape=jax.ShapeDtypeStruct(acc.shape, F32),
        compiler_params=pltpu.CompilerParams(vmem_limit_bytes=56 * 1024 * 1024),
        cost_estimate=contract_cost(1, w.shape[0], n, q.shape[2] // 2),
        name="contract_near",
    )(table, sink, t, q, w, acc)


def after(value, *others):
    return lax.optimization_barrier((value, *others))[0]


def rows_to_send(perambulators, source_times):
    position, srcs = lax.axis_index("src"), lax.axis_size("src")
    held = perambulators.shape[0]
    out = []
    for k in range(1, srcs):
        to = lax.rem(position + srcs - k, srcs)
        within = lax.dynamic_index_in_dim(source_times, to, 0, keepdims=False) - position * held
        out.append(lax.dynamic_index_in_dim(perambulators, jnp.clip(within, 0, held - 1), 0, keepdims=False))
    return out


def own_rows(sent, held, source_times):
    position, srcs = lax.axis_index("src"), lax.axis_size("src")
    own_time = lax.dynamic_index_in_dim(source_times, position, 0, keepdims=False)
    chosen = None
    for k in range(1, srcs):
        got = lax.ppermute(sent[k - 1], "src", [(j, (j + srcs - k) % srcs) for j in range(srcs)])
        here = own_time // held == lax.rem(position + k, srcs)
        chosen = got if chosen is None else jnp.where(here, got, chosen)
    return chosen


def all_rows(rows):
    return lax.all_gather(rows, "ev", axis=2, tiled=True)


def maps_kernel(at_ref, *refs, sources, chunks, stride, e):
    times, (left_ref, right_ref, *middle_refs, turned) = refs[:sources], refs[sources:]
    _, parts, n, _ = times[0].shape
    structures = right_ref.shape[0] // sources
    size = left_ref.shape[1] // (structures * 2 * chunks)
    start = at_ref[3 * structures]
    for g in range(sources):
        for s in range(structures):
            first, second, third = (times[g].at[at_ref[3 * s + k]] for k in range(3))
            for k in range(chunks):
                rows = pl.ds(pl.multiple_of(start + k * stride, size), size)
                re, im = first[0, rows, :], first[1, rows, :]
                for part, (x, y) in enumerate(((re, im), (im, -re))):
                    to = ((s * 2 + part) * chunks + k) * size
                    left_ref[g, to : to + size, :n] = x
                    left_ref[g, to : to + size, n:] = y
            c = g * structures + s
            re, im = third[0], third[1]
            right_ref[c, 0, :, :n] = re
            right_ref[c, 0, :, n:] = im
            right_ref[c, 1, :, :n] = -im
            right_ref[c, 1, :, n:] = re
            for part in range(parts):
                turned[part] = second[part].astype(F32).T
            for k, middle_ref in enumerate(middle_refs):
                columns = pl.ds(pl.multiple_of(at_ref[3 * structures + 1 + k], e), e)
                re, im = turned[0, columns, :], turned[1, columns, :]
                middle_ref[c, 0] = jnp.concatenate([re, im], 0).astype(BF16)
                middle_ref[c, 1] = jnp.concatenate([-im, re], 0).astype(BF16)


def maps(times, spin_index, first_row, chunks, size, stride, e, places):
    n = times[0].shape[2]
    structures, sources = spin_index.shape[0], len(times)
    combos = sources * structures
    at = jnp.concatenate([spin_index.reshape(-1), scalars(first_row, *places)])
    shapes = [(sources, structures * 2 * chunks * size, 2 * n), (combos, 2, n, 2 * n)] + [(combos, 2, 2 * e, n)] * len(places)
    return pl.pallas_call(
        functools.partial(maps_kernel, sources=sources, chunks=chunks, stride=stride, e=e),
        grid_spec=pltpu.PrefetchScalarGridSpec(
            num_scalar_prefetch=1,
            grid=(1,),
            in_specs=[whole(t) for t in times],
            out_specs=[pl.BlockSpec(shape, lambda i, at, d=len(shape): (0,) * d) for shape in shapes],
            scratch_shapes=[pltpu.VMEM((2, n, n), F32)],
        ),
        out_shape=[jax.ShapeDtypeStruct(shape, BF16) for shape in shapes],
        compiler_params=pltpu.CompilerParams(vmem_limit_bytes=48 * 1024 * 1024),
        name="maps",
    )(at, *times)


def body_any(sink_tensor, source_tensor, perambulators, source_times, spin_index):
    position, ev = lax.axis_index("src"), lax.axis_index("ev")
    evs, srcs = lax.axis_size("ev"), lax.axis_size("src")
    structures = spin_index.shape[0]
    _, slice_a, n, _ = sink_tensor.shape
    e = n // evs
    share = slice_a // srcs
    mine = lax.dynamic_slice_in_dim(sink_tensor, position * share, share, axis=1)
    sink = lax.all_gather(mine, ("ev", "src"), axis=1, tiled=True)
    sent = rows_to_send(perambulators, source_times)
    per_time = all_rows(own_rows(sent, perambulators.shape[0], source_times))
    left, w, q = maps([per_time], spin_index, 0, 1, n, n, e, [ev * e])
    t = project_source(left[0], source_tensor[0], structures)
    acc = jnp.zeros((structures, 2, n // LANES, 8, LANES), F32)
    acc = contract(sink, [t], scalars(0, 0, 1), 0, q, w, acc, n // BLOCK)
    return lax.psum(acc.sum((2, 3, 4)), "ev")


RELAY_CALLS = (
    (
        (("near", "u0"), None, 1),
        (None, ("opposite", "u0"), 1),
        (("near", "p0"), ("opposite", "p0"), 1),
    ),
    (
        (("across", "u0"), ("near", "u0"), 2),
        (None, ("opposite", "u1"), 1),
    ),
    (
        (("across", "p0"), ("near", "p0"), 1),
        (("across", "u1"), ("near", "u1"), 2),
    ),
    (
        (("opposite", "u0"), ("across", "u0"), 2),
        (("across", "p1"), ("opposite", "p1"), 1),
    ),
    (
        (None, ("near", "u2"), 1),
        (("opposite", "p0"), ("across", "p0"), 1),
        (("opposite", "u1"), ("across", "u1"), 2),
    ),
    ((("opposite", "p1"), ("across", "p1"), 2),),
)
OWN_TABLE = 10
BASES = tuple(OWN_TABLE + 2 * sum(len(call) for call in RELAY_CALLS[:k]) for k in range(len(RELAY_CALLS)))


def relay_table(evs, units):
    rows = []
    for ev in range(evs):
        for position in range(4):
            for grp in range(2):
                chip, core = position // 2, position % 2
                end = int(ev in (0, evs - 1))
                near = 1 - ev if ev < 2 else 5 - ev
                slices = dict(near=near, opposite=3 - ev, across=3 - near)
                unit = {f"u{w}": units - 1 - w if chip else w for w in range(units)}
                unit |= {f"p{w}": w if chip else units - 1 - w for w in range(units)}
                row = [core * units, ev * units, 1]
                row += [core * units + units // 2, ev * units + units // 2, 1]
                row += [core * units + 1 + grp, 1 - end, core * units + 2 - grp, 1 - end]
                for call in RELAY_CALLS:
                    for at_end, at_inner, choices in call:
                        at = at_end if end else at_inner
                        which = 0 if at is None else 1 if end or choices == 1 else 2
                        row += [which, 0 if at is None else slices[at[0]] * units + unit[at[1]]]
                rows.append(row)
    return np.array(rows, np.int32)


def body_relay(sink_tensor, source_tensor, perambulators, source_times, spin_index):
    position, ev, grp = lax.axis_index("src"), lax.axis_index("ev"), lax.axis_index("grp")
    evs, srcs = lax.axis_size("ev"), lax.axis_size("src")
    structures = spin_index.shape[0]
    _, slice_a, n, _ = sink_tensor.shape
    e = n // evs
    chip, core = position // 2, position % 2
    half = slice_a // 2
    units = half // BLOCK
    is_end = (ev == 0) | (ev == evs - 1)
    near = jnp.where(ev < 2, 1 - ev, 5 - ev)

    def unit(w):
        return jnp.where(chip == 0, w, units - 1 - w)

    def own(w, start=0, size=BLOCK):
        return lax.dynamic_slice_in_dim(sink_tensor, core * half + BLOCK * unit(w) + start, size, axis=1)

    outward = lambda v: lax.ppermute(v, "ev", [(1, 0), (2, 3)])
    inward = lambda v: lax.ppermute(v, "ev", [(0, 1), (3, 2)])
    middle = lambda v: lax.ppermute(v, "ev", [(1, 2), (2, 1)])
    swap_chips = lambda v: lax.ppermute(v, "src", [(0, 2), (2, 0), (1, 3), (3, 1)])
    swap_cores = lambda v: lax.ppermute(v, "src", [(0, 1), (1, 0), (2, 3), (3, 2)])
    swap_groups = lambda v: lax.ppermute(v, "grp", [(0, 1), (1, 0)])

    table = jnp.asarray(relay_table(evs, units))
    table = lax.dynamic_index_in_dim(table, (ev * 4 + position) * 2 + grp, 0, keepdims=False)
    base1, base2, base3, base4, base5, base6 = BASES

    choose = lambda a, b: jnp.where(is_end, a, b)

    sent = rows_to_send(perambulators, source_times)
    rows_here = own_rows(sent, perambulators.shape[0], source_times)
    spins = rows_here.shape[0]
    small = BLOCK // 4
    own0s, own0r, own2a, own2b = own(0, 0, small), own(0, small, BLOCK - small), own(2, 0, BLOCK // 2), own(2, BLOCK // 2, BLOCK // 2)
    own0, own1 = own(0), own(1)
    rows_here = after(rows_here, own0s, own0r, own2a, own2b, own0, own1)
    some = lax.dynamic_slice_in_dim(rows_here, grp * (spins // 2), spins // 2, axis=0)
    mine = jnp.stack([lax.ppermute(some, "ev", [(j, (j + k) % evs) for j in range(evs)]) for k in range(1, evs)])
    q1s, b1s, e1a = outward(own0s), middle(own0s), inward(own2a)
    others = swap_groups(after(mine, q1s, b1s))
    q1r, b1r, e2, b3 = outward(own0r), middle(own0r), inward(own0), middle(own1)
    whole_rows = jnp.where(grp == 0, jnp.concatenate([mine, others], 1), jnp.concatenate([others, mine], 1))
    whole_rows = [rows_here if k == 0 else whole_rows[k - 1] for k in range(evs)]
    turned = jnp.stack([whole_rows[(evs - 1 - k) % evs] for k in range(2 * evs - 1)])
    turned = lax.dynamic_slice_in_dim(turned, evs - 1 - ev, evs, axis=0)
    per_time = turned.transpose(1, 2, 0, 3, 4).reshape(spins, 2, n, n)
    other_time = swap_cores(per_time)
    source = source_tensor[0]
    other_source = swap_cores(after(source, rows_here))
    lefts, w, q, q_near = maps(
        [per_time, other_time], spin_index, core * half, evs, half, slice_a, e, [ev * e, near * e]
    )
    acc = jnp.zeros((2 * structures, 2, n // LANES, 8, LANES), F32)
    join = lambda *parts: jnp.concatenate(parts, 1)

    t_own = project_source(lefts[0], source, structures)
    q1r, b1r = after((q1r, b1r), t_own)
    b1, q1 = join(b1s, b1r), join(q1s, q1r)
    q2 = outward(b1)
    x1 = swap_chips(choose(q1, b1))
    e3, e1b = inward(after(own1, t_own)), inward(after(own2b, t_own))
    t_other = project_source(lefts[1], after(other_source, t_own, b1, q1), structures)
    ts = (t_own, t_other)
    block = near * units + 1 + grp
    to_near = jnp.stack([lax.dynamic_slice_in_dim(t, block * BLOCK, BLOCK, axis=4) for t in ts]).astype(BF16)
    near_t = inward(to_near.reshape(to_near.shape[:4] + (e * BLOCK, LANES)))
    acc = contract(sink_tensor, ts, table, 0, q, w, acc, units // 2)
    q3 = outward(after(b3, acc))
    x2 = swap_chips(choose(after(q2, acc), e2))
    b2 = middle(after(e2, acc))
    acc = contract(sink_tensor, ts, table, 3, q, w, after(acc, b3, q2, e2), units // 2)
    acc = contract_slots([[(q1,)], [(b1,)], [(x1,)]], ts, table, base1, q, w, acc)
    q4 = outward(after(b2, acc))
    x3 = swap_chips(choose(after(q3, acc), b3))
    b4 = middle(after(e3, acc))
    b5 = middle(after(e1a, acc))
    acc = contract_slots([[(q2,), (e2,)], [(b3,)]], ts, table, base2, q, w, after(acc, b2, q3, e3))
    far_t = swap_groups(after(near_t, acc))
    acc = contract_slots([[(x2,)], [(q3,), (e3,)]], ts, table, base3, q, w, after(acc, near_t))
    q5 = outward(after(b4, acc))
    x4 = swap_chips(choose(after(q4, acc), b2))
    acc = contract_near(sink_tensor, near_t, table, 6, q_near, w, after(acc, b4, q4))
    q6 = outward(after(b5, acc))
    acc = contract_near(sink_tensor, far_t, table, 8, q_near, w, after(acc, b5))
    acc = contract_slots([[(q4,), (b2,)], [(x3,)]], ts, table, base4, q, w, acc)
    x5 = swap_chips(choose(after(q5, acc), b4)[:, BLOCK // 2 :])
    acc = contract_slots([[(e1a, e1b)], [(x4,)], [(q5,), (b4,)]], ts, table, base5, q, w, after(acc, q5))
    acc = contract_slots([[(q6, x5), (b5, x5)]], ts, table, base6, q, w, acc)

    part = acc.sum((2, 3, 4)).reshape(2, structures, 2)
    total = part[0] + swap_cores(part[1])
    return lax.psum(total, "ev")


def body(relay, *args):
    totals = (body_relay if relay else body_any)(*args)
    return (totals * float(args[0].shape[3]) ** -1.5)[None]


def solution(mesh):
    relay = mesh.shape["ev"] == 4 and mesh.shape["src"] == 4 and mesh.shape["grp"] == 2
    in_specs = (
        P("grp", "ev", None, None),
        P("src", None, None, "ev", None),
        P("src", None, None, "ev", None),
        P(),
        P(),
    )
    out_specs = P("src", "grp", None)
    return jax.shard_map(functools.partial(body, relay), mesh=mesh, in_specs=in_specs, out_specs=out_specs, check_vma=False)
```

time: 1060 us -> 409 us (0.39)
  waiting for transfers between devices: 557 us -> 45.6 us
  matrix products: 308 us -> 0 us
  Pallas kernels: 0 us -> 199 us
  local copies, waits for them, and re-layouts: 116 us -> 28.1 us
  starting transfers between devices: 14.8 us -> 86.8 us
  between operations: 27.7 us -> 5.24 us
  blocking collectives: 10.4 us -> 23.9 us
    all_to_all x2 -> x0, waiting for transfers between devices: 518 us -> none  [body(): lax.all_to_all(projected, 'ev', split_axis=2, concat_axis=1, tiled=True)]
    dot_general x24 -> x0, matrix products: 308 us -> none  [the longest x6 107 us: apply_mode(): jnp.einsum(pattern, tensor[1], matrix[1], preferred_element_type=jnp.floa...]
    pallas_call x0 -> x13, Pallas kernels: none -> 199 us  [the longest x6 106 us: contract_slots(): pl.pallas_call(functools.partial(slots_kernel, sources=len(ts), shapes=sh...]
    ppermute x0 -> x34, starting transfers between devices: none -> 86.8 us  [the longest x5 38.4 us: body_relay(): inward = lambda v: lax.ppermute(v, 'ev', [(0, 1), (3, 2)])]
    ppermute x0 -> x34, waiting for transfers between devices: none -> 45.6 us  [the longest x5 14.7 us: body_relay(): lax.ppermute(v, 'src', [(0, 2), (2, 0), (1, 3), (3, 1)])]
    another operation x2 -> x3, local copies, waits for them, and re-layouts: 48.4 us -> 3.52 us  [the longest x2 3.51 us: body_relay(): jnp.stack([lax.dynamic_slice_in_dim(t, block * BLOCK, BLOCK, axis=4) for...]
    all_gather x2 -> x0, waiting for transfers between devices: 38.6 us -> none  [the longest x1 23.7 us: body(): every_time = lax.all_gather(perambulators, 'src', axis=0, tiled=True)]
    slice x5 -> x1, local copies, waits for them, and re-layouts: 34.3 us -> 0.01 us  [body_relay(): total = part[0] + swap_cores(part[1])]
  transfers between devices with their start and end apart: 4 -> 34, of which waited for: 4 -> 10; matrix products, arithmetic and copies ran while one was open for 20% -> 8% of each run, Pallas kernels for 0% -> 46%
where the time goes in v2:
time: 409 us; the launch traced here: 402 us
  Pallas kernels  199 us (49%)
  starting transfers between devices  86.8 us (21%)
  waiting for transfers between devices  45.6 us (11%)
  local copies, waits for them, and re-layouts  28.1 us (7%)
  blocking collectives  23.9 us (6%)
  other arithmetic  13.1 us (3%)
  between operations  5.24 us (1%)
    pallas_call x6, Pallas kernels, contract_slots(): pl.pallas_call(functools.partial(slots_kernel, sources=len(ts), shapes=sh...  106 us
    pallas_call x2, Pallas kernels, project_source(): pl.pallas_call(project_kernel, grid=(e // per,), in_specs=[pl.BlockSpec(l...  46 us
    ppermute x5, starting transfers between devices, body_relay(): inward = lambda v: lax.ppermute(v, 'ev', [(0, 1), (3, 2)])  38.4 us
    pallas_call x2, Pallas kernels, contract(): pl.pallas_call(functools.partial(contract_kernel, sources=len(ts), base=b...  35.9 us
    psum x1, blocking collectives, body_relay(): return lax.psum(total, 'ev')  23.9 us
    ppermute x3, starting transfers between devices, body_relay(): lax.ppermute(some, 'ev', [(j, (j + k) % evs) for j in range(evs)])  16.7 us
    ppermute x5, waiting for transfers between devices, body_relay(): lax.ppermute(v, 'src', [(0, 2), (2, 0), (1, 3), (3, 1)])  14.7 us
    ppermute x3, waiting for transfers between devices, body_relay(): lax.ppermute(some, 'ev', [(j, (j + k) % evs) for j in range(evs)])  13.5 us
  transfers between devices with their start and end apart: 34, of which 10 were waited for; matrix products, arithmetic and copies ran while one was open for 8% of the time, Pallas kernels for 46%

profile of v2, /device:TPU:0, one launch (start us, length us, event | category | flops | bytes accessed | tf_op | source)
XLA Modules:
  0.0 401.7 jit_solution(3367422849736236263)
XLA Ops:
  18.5 4.7 %constant_dynamic-slice_fusion.2 = (bf16[2,8,256,256]{3,2,1,0:T(8,128)(2,1)}, bf16[2,8,256,256]{3,2,1,0:T(8,128)(2,1)}) fusion(bf16[2,64,256,256]{3,2,1,0:T(8,128)(2,1)} %sink_ref.7, s32[]{:T(128)S(6)} %select_n.145, s32[]{:T(128)S(6)} %select_n.130), kind=kLoop, calls=%fused_computation.31 | loop fusion | bytes 8388616 | tf_op jit(solution)/shard_map/dynamic_slice | solution.py:407
  25.4 6.6 %collective-permute-start.7 = (bf16[2,2,64,256]{3,2,1,0:T(8,128)(2,1)S(1)}, bf16[2,2,64,256]{3,2,1,0:T(8,128)(2,1)S(1)}, u32[]{:S(2)}, u32[]{:S(2)}) collective-permute-start(bf16[2,2,64,256]{3,2,1,0:T(8,128)(2,1)S(1)} %constant_dynamic-slice_fusion.1), channel_id=1, source_target_pairs={{0,4},{4,8},{8,12},{12,0},{1,5},{5,9},{9,13},{13,1},{2,6},{6,10},{... | collective-permute-start | bytes 393224 | tf_op jit(solution)/shard_map/ppermute | solution.py:430
  35.9 10.0 %collective-permute-start.9 = (bf16[2,2,64,256]{3,2,1,0:T(8,128)(2,1)S(1)}, bf16[2,2,64,256]{3,2,1,0:T(8,128)(2,1)S(1)}, u32[]{:S(2)}, u32[]{:S(2)}) collective-permute-start(bf16[2,2,64,256]{3,2,1,0:T(8,128)(2,1)S(1)} %constant_dynamic-slice_fusion.1), channel_id=1, source_target_pairs={{0,12},{4,0},{8,4},{12,8},{1,13},{5,1},{9,5},{13,9},{2,14},{6,2},{... | collective-permute-start | bytes 393224 | tf_op jit(solution)/shard_map/ppermute | solution.py:430
  50.1 5.5 %collective-permute-done.9 = bf16[2,2,64,256]{3,2,1,0:T(8,128)(2,1)S(1)} collective-permute-done((bf16[2,2,64,256]{3,2,1,0:T(8,128)(2,1)S(1)}, bf16[2,2,64,256]{3,2,1,0:T(8,128)(2,1)S(1)}, u32[]{:S(2)}, u32[]{:S(2)}) %collective-permute-start.9) | collective-permute-done | bytes 131104 | tf_op jit(solution)/shard_map/ppermute | solution.py:430
  57.2 7.3 %collective-permute-done.11 = bf16[3,2,2,64,256]{4,3,0,2,1:T(8,128)(2,1)S(1)} collective-permute-done((bf16[3,2,2,64,256]{4,3,0,2,1:T(8,128)(2,1)S(1)}, bf16[3,2,2,64,256]{4,3,0,2,1:T(8,128)(2,1)S(1)}, u32[]{:S(2)}, u32[]{:S(2)}) %collective-permute-start.11) | collective-permute-done | bytes 393248 | tf_op jit(solution)/shard_map/ppermute | solution.py:414
  68.2 9.8 %collective-permute-start.17 = (bf16[2,8,256,256]{3,2,1,0:T(8,128)(2,1)}, bf16[2,8,256,256]{3,2,1,0:T(8,128)(2,1)}, u32[]{:S(2)}, u32[]{:S(2)}) collective-permute-start(bf16[2,8,256,256]{3,2,1,0:T(8,128)(2,1)} %get-tuple-element.66), channel_id=1, source_target_pairs={{0,4},{12,8},{1,5},{13,9},{2,6},{14,10},{3,7},{15,11},{16,20},{28,... | collective-permute-start | bytes 6291464 | tf_op jit(solution)/shard_map/ppermute | solution.py:410
  86.5 23.0 %project_source.2.refs_0_.refs_3_.refs_5_.refs_4_ = f32[2,2,2,64,128,128]{5,4,3,2,1,0:T(8,128)} custom-call(bf16[512,512]{1,0:T(8,128)(2,1)} %get-tuple-element.70.left_ref, bf16[2,256,64,256]{3,2,1,0:T(8,128)(2,1)} %bitcast.43), custom_call_target="tpu_custom_call" | custom-call | flops 8589934592 | bytes 50331648 | tf_op jit(solution)/shard_map/project_source/pallas_call | solution.py:38
  118.2 6.2 %collective-permute-start.22 = (bf16[2,8,256,256]{3,2,1,0:T(8,128)(2,1)}, bf16[2,8,256,256]{3,2,1,0:T(8,128)(2,1)}, u32[]{:S(2)}, u32[]{:S(2)}) collective-permute-start(bf16[2,8,256,256]{3,2,1,0:T(8,128)(2,1)} %get-tuple-element.49), channel_id=1, source_target_pairs={{0,4},{12,8},{1,5},{13,9},{2,6},{14,10},{3,7},{15,11},{16,20},{28,... | collective-permute-start | bytes 6291464 | tf_op jit(solution)/shard_map/ppermute | solution.py:410
  124.3 23.0 %project_source.3.refs_1_.refs_4_.refs_6_.refs_5_ = f32[2,2,2,64,128,128]{5,4,3,2,1,0:T(8,128)} custom-call(bf16[512,512]{1,0:T(8,128)(2,1)} %get-tuple-element.69.left_ref, bf16[2,256,64,256]{3,2,1,0:T(8,128)(2,1)} %collective-permute-done.14.source_ref), custom_call_target="tpu_custom_call" | custom-call | flops 8589934592 | bytes 50331648 | tf_op jit(solution)/shard_map/project_source/pallas_call | solution.py:38
  147.9 18.0 %contract.2.refs_4_ = f32[4,2,2,8,128]{4,3,2,1,0:T(8,128)} custom-call(s32[36]{0:T(128)} %fusion.2.at_ref, bf16[2,64,256,256]{3,2,1,0:T(8,128)(2,1)} %sink_ref.7, f32[2,2,2,64,128,128]{5,4,3,2,1,0:T(8,128)} %project_source.2.refs_0_.refs_3_.refs_5_.refs_4_, f32[2,2,2,64,128,128]{5,4,3,2,1,0:T(8,128)} %project_source.3.refs_1_.refs_4_.refs_6_.refs_5_, ...), custom_call_target="tpu_custom_call" | custom-call | flops 10737418240 | bytes 12582912 | tf_op jit(solution)/shard_map/contract/pallas_call | solution.py:131
  170.7 17.9 %contract.3.refs_7_ = f32[4,2,2,8,128]{4,3,2,1,0:T(8,128)} custom-call(s32[36]{0:T(128)} %fusion.2.at_ref, bf16[2,64,256,256]{3,2,1,0:T(8,128)(2,1)} %sink_ref.7, f32[2,2,2,64,128,128]{5,4,3,2,1,0:T(8,128)} %project_source.2.refs_0_.refs_3_.refs_5_.refs_4_, f32[2,2,2,64,128,128]{5,4,3,2,1,0:T(8,128)} %project_source.3.refs_1_.refs_4_.refs_6_.refs_5_, ...), custom_call_target="tpu_custom_call" | custom-call | flops 10737418240 | bytes 12582912 | tf_op jit(solution)/shard_map/contract/pallas_call | solution.py:131
  193.6 7.6 %collective-permute-start.19 = (bf16[2,2,2,2,512,128]{5,4,3,2,1,0:T(8,128)(2,1)}, bf16[2,2,2,2,512,128]{5,4,3,2,1,0:T(8,128)(2,1)}, u32[]{:S(2)}, u32[]{:S(2)}) collective-permute-start(bf16[2,2,2,2,512,128]{5,4,3,2,1,0:T(8,128)(2,1)} %pad_maximum_fusion), channel_id=1, source_target_pairs={{0,4},{12,8},{1,5},{13,9},{2,6},{14,10},{3,7},{15,11},{16,20},{28,... | collective-permute-start | bytes 6291464 | tf_op jit(solution)/shard_map/ppermute | solution.py:410
  202.7 22.4 %contract_slots.6.refs_7_ = f32[4,2,2,8,128]{4,3,2,1,0:T(8,128)} custom-call(s32[36]{0:T(128)} %fusion.2.at_ref, bf16[2,8,256,256]{3,2,1,0:T(8,128)(2,1)} %copy-done.2, bf16[2,8,256,256]{3,2,1,0:T(8,128)(2,1)} %copy-done.3, bf16[2,8,256,256]{3,2,1,0:T(8,128)(2,1)} %collective-permute-done.13.refs_2_, ...), custom_call_target="tpu_custom_call" | custom-call | flops 16106127360 | bytes 18874368 | tf_op jit(solution)/shard_map/contract_slots/pallas_call | solution.py:191
  229.3 13.0 %contract_slots.7.refs_7_ = f32[4,2,2,8,128]{4,3,2,1,0:T(8,128)} custom-call(s32[36]{0:T(128)} %fusion.2.at_ref, bf16[2,8,256,256]{3,2,1,0:T(8,128)(2,1)} %copy-done.5, bf16[2,8,256,256]{3,2,1,0:T(8,128)(2,1)} %collective-permute-done.17.refs_1_, bf16[2,8,256,256]{3,2,1,0:T(8,128)(2,1)} %collective-permute-done.15.refs_2_, ...), custom_call_target="tpu_custom_call" | custom-call | flops 10737418240 | bytes 12582912 | tf_op jit(solution)/shard_map/contract_slots/pallas_call | solution.py:191
  248.8 19.5 %contract_slots.8.acc_ref = f32[4,2,2,8,128]{4,3,2,1,0:T(8,128)} custom-call(s32[36]{0:T(128)} %fusion.2.at_ref, bf16[2,8,256,256]{3,2,1,0:T(8,128)(2,1)} %collective-permute-done.20.refs_0_, bf16[2,8,256,256]{3,2,1,0:T(8,128)(2,1)} %copy-done.6, bf16[2,8,256,256]{3,2,1,0:T(8,128)(2,1)} %collective-permute-done.22.refs_2_, ...), custom_call_target="tpu_custom_call" | custom-call | flops 10737418240 | bytes 12582912 | tf_op jit(solution)/shard_map/contract_slots/pallas_call | solution.py:191
  270.0 5.2 %collective-permute-done.25.refs_0_ = bf16[2,8,256,256]{3,2,1,0:T(8,128)(2,1)S(1)} collective-permute-done((bf16[2,8,256,256]{3,2,1,0:T(8,128)(2,1)S(1)}, bf16[2,8,256,256]{3,2,1,0:T(8,128)(2,1)S(1)}, u32[]{:S(2)}, u32[]{:S(2)}) %collective-permute-start.25) | collective-permute-done | bytes 2097184 | tf_op jit(solution)/shard_map/ppermute | solution.py:409
  277.8 4.3 %contract_near.2.acc_ref = f32[4,2,2,8,128]{4,3,2,1,0:T(8,128)} custom-call(s32[36]{0:T(128)} %fusion.2.at_ref, bf16[2,64,256,256]{3,2,1,0:T(8,128)(2,1)} %sink_ref.7, bf16[2,2,2,2,512,128]{5,4,3,2,1,0:T(8,128)(2,1)} %collective-permute-done.19.t_ref, bf16[4,2,128,256]{3,2,1,0:T(8,128)(2,1)} %copy-done.1, ...), custom_call_target="tpu_custom_call" | custom-call | flops 5368709120 | bytes 6291456 | tf_op jit(solution)/shard_map/contract_near/pallas_call | solution.py:223
  282.1 12.6 %collective-permute-start.31 = (bf16[2,4,256,256]{3,2,1,0:T(8,128)(2,1)S(1)}, bf16[2,4,256,256]{3,2,1,0:T(8,128)(2,1)S(1)}, u32[]{:S(2)}, u32[]{:S(2)}) collective-permute-start(bf16[2,4,256,256]{3,2,1,0:T(8,128)(2,1)S(1)} %copy-done.13), channel_id=1, source_target_pairs={{0,4},{12,8},{1,5},{13,9},{2,6},{14,10},{3,7},{15,11},{16,20},{28,... | collective-permute-start | bytes 3145736 | tf_op jit(solution)/shard_map/ppermute | solution.py:410
  294.8 4.2 %contract_near.3.refs_7_ = f32[4,2,2,8,128]{4,3,2,1,0:T(8,128)} custom-call(s32[36]{0:T(128)} %fusion.2.at_ref, bf16[2,64,256,256]{3,2,1,0:T(8,128)(2,1)} %sink_ref.7, bf16[2,2,2,2,512,128]{5,4,3,2,1,0:T(8,128)(2,1)} %collective-permute-done.29.t_ref, bf16[4,2,128,256]{3,2,1,0:T(8,128)(2,1)} %copy-done.1, ...), custom_call_target="tpu_custom_call" | custom-call | flops 5368709120 | bytes 6291456 | tf_op jit(solution)/shard_map/contract_near/pallas_call | solution.py:223
  299.0 19.5 %contract_slots.9.refs_9_ = f32[4,2,2,8,128]{4,3,2,1,0:T(8,128)} custom-call(s32[36]{0:T(128)} %fusion.2.at_ref, bf16[2,8,256,256]{3,2,1,0:T(8,128)(2,1)} %copy-done.7, bf16[2,8,256,256]{3,2,1,0:T(8,128)(2,1)} %copy-done.4, bf16[2,8,256,256]{3,2,1,0:T(8,128)(2,1)} %collective-permute-done.28.refs_2_, ...), custom_call_target="tpu_custom_call" | custom-call | flops 10737418240 | bytes 12582912 | tf_op jit(solution)/shard_map/contract_slots/pallas_call | solution.py:191
  326.9 14.2 %collective-permute-done.32.refs_2_ = bf16[2,8,256,256]{3,2,1,0:T(8,128)(2,1)} collective-permute-done((bf16[2,8,256,256]{3,2,1,0:T(8,128)(2,1)}, bf16[2,8,256,256]{3,2,1,0:T(8,128)(2,1)}, u32[]{:S(2)}, u32[]{:S(2)}) %collective-permute-start.32) | collective-permute-done | bytes 2097184 | tf_op jit(solution)/shard_map/ppermute | solution.py:412
  341.1 19.5 %contract_slots.10.refs_8_ = f32[4,2,2,8,128]{4,3,2,1,0:T(8,128)} custom-call(s32[36]{0:T(128)} %fusion.2.at_ref, bf16[2,4,256,256]{3,2,1,0:T(8,128)(2,1)} %collective-permute-done.refs_0_, bf16[2,4,256,256]{3,2,1,0:T(8,128)(2,1)} %copy-done.11, bf16[2,8,256,256]{3,2,1,0:T(8,128)(2,1)} %collective-permute-done.32.refs_2_, ...), custom_call_target="tpu_custom_call" | custom-call | flops 16106127360 | bytes 18874368 | tf_op jit(solution)/shard_map/contract_slots/pallas_call | solution.py:191
  362.6 12.3 %contract_slots.11 = f32[4,2,2,8,128]{4,3,2,1,0:T(8,128)} custom-call(s32[36]{0:T(128)} %fusion.2.at_ref, bf16[2,4,256,256]{3,2,1,0:T(8,128)(2,1)} %copy-done.12, bf16[2,4,256,256]{3,2,1,0:T(8,128)(2,1)} %copy-done.9, bf16[2,4,256,256]{3,2,1,0:T(8,128)(2,1)} %copy-done.10, bf16[2,4,256,256]{3,2,1,0:T(8,128)(2,1)} %copy-done.9, ...), custom_call_target="tpu_custom_call" | custom-call | flops 5368709120 | bytes 6291456 | tf_op jit(solution)/shard_map/contract_slots/pallas_call | solution.py:191
  377.0 23.9 %psum.7 = f32[2,2]{1,0:T(2,128)S(1)} all-reduce(f32[2,2]{1,0:T(2,128)S(1)} %slice_add_fusion), channel_id=1, replica_groups=mesh['grp'=2,'ev'=4,'src'=4] {'ev'}, use_global_device_ids=true, to_apply=%region_1.2 | all-reduce | flops 4 | bytes 32 | tf_op jit(solution)/shard_map/psum | solution.py:484
  (127 shorter events, 86.2 us)
Async XLA Ops:
  23.3 94.9 %collective-permute-start.14 = (bf16[2,256,64,256]{3,2,1,0:T(8,128)(2,1)}, bf16[2,256,64,256]{3,2,1,0:T(8,128)(2,1)}, u32[]{:S(2)}, u32[]{:S(2)}) collective-permute-start(bf16[2,256,64,256]{3,2,1,0:T(8,128)(2,1)} %bitcast.42), channel_id=1, source_target_pairs={{0,1},{1,0},{2,3},{3,2},{4,5},{5,4},{6,7},{7,6},{8,9},{9,8},{10,11... | collective-permute-start | bytes 50331656 | tf_op jit(solution)/shard_map/ppermute | solution.py:413
  23.4 32.3 %collective-permute-start.1 = (bf16[2,2,256,256]{3,2,1,0:T(8,128)(2,1)S(1)}, bf16[2,2,256,256]{3,2,1,0:T(8,128)(2,1)S(1)}, u32[]{:S(2)}, u32[]{:S(2)}) collective-permute-start(bf16[2,2,256,256]{3,2,1,0:T(8,128)(2,1)S(1)} %constant_dynamic-slice_fusion.6), channel_id=1, source_target_pairs={{4,0},{8,12},{5,1},{9,13},{6,2},{10,14},{7,3},{11,15},{20,16},{24,... | collective-permute-start | bytes 1572872 | tf_op jit(solution)/shard_map/ppermute | solution.py:409
  65.0 44.5 %collective-permute-start.2 = (bf16[2,6,256,256]{3,2,1,0:T(8,128)(2,1)}, bf16[2,6,256,256]{3,2,1,0:T(8,128)(2,1)}, u32[]{:S(2)}, u32[]{:S(2)}) collective-permute-start(bf16[2,6,256,256]{3,2,1,0:T(8,128)(2,1)} %constant_dynamic-slice_fusion.5), channel_id=1, source_target_pairs={{4,0},{8,12},{5,1},{9,13},{6,2},{10,14},{7,3},{11,15},{20,16},{24,... | collective-permute-start | bytes 4718600 | tf_op jit(solution)/shard_map/ppermute | solution.py:409
  66.3 43.2 %collective-permute-start.3 = (bf16[2,6,256,256]{3,2,1,0:T(8,128)(2,1)}, bf16[2,6,256,256]{3,2,1,0:T(8,128)(2,1)}, u32[]{:S(2)}, u32[]{:S(2)}) collective-permute-start(bf16[2,6,256,256]{3,2,1,0:T(8,128)(2,1)} %constant_dynamic-slice_fusion.5), channel_id=1, source_target_pairs={{4,8},{8,4},{5,9},{9,5},{6,10},{10,6},{7,11},{11,7},{20,24},{24,20... | collective-permute-start | bytes 4718600 | tf_op jit(solution)/shard_map/ppermute | solution.py:411
  68.2 97.7 %collective-permute-start.17 = (bf16[2,8,256,256]{3,2,1,0:T(8,128)(2,1)}, bf16[2,8,256,256]{3,2,1,0:T(8,128)(2,1)}, u32[]{:S(2)}, u32[]{:S(2)}) collective-permute-start(bf16[2,8,256,256]{3,2,1,0:T(8,128)(2,1)} %get-tuple-element.66), channel_id=1, source_target_pairs={{0,4},{12,8},{1,5},{13,9},{2,6},{14,10},{3,7},{15,11},{16,20},{28,... | collective-permute-start | bytes 6291464 | tf_op jit(solution)/shard_map/ppermute | solution.py:410
  79.4 88.8 %collective-permute-start.15 = (bf16[2,8,256,256]{3,2,1,0:T(8,128)(2,1)}, bf16[2,8,256,256]{3,2,1,0:T(8,128)(2,1)}, u32[]{:S(2)}, u32[]{:S(2)}) collective-permute-start(bf16[2,8,256,256]{3,2,1,0:T(8,128)(2,1)} %get-tuple-element.49), channel_id=1, source_target_pairs={{4,8},{8,4},{5,9},{9,5},{6,10},{10,6},{7,11},{11,7},{20,24},{24,20... | collective-permute-start | bytes 6291464 | tf_op jit(solution)/shard_map/ppermute | solution.py:411
  111.1 57.9 %collective-permute-start.16 = (bf16[2,8,256,256]{3,2,1,0:T(8,128)(2,1)S(1)}, bf16[2,8,256,256]{3,2,1,0:T(8,128)(2,1)S(1)}, u32[]{:S(2)}, u32[]{:S(2)}) collective-permute-start(bf16[2,8,256,256]{3,2,1,0:T(8,128)(2,1)S(1)} %constant_dynamic-update-slice_fusion.2.refs_1_), channel_id=1, source_target_pairs={{4,0},{8,12},{5,1},{9,13},{6,2},{10,14},{7,3},{11,15},{20,16},{24,... | collective-permute-start | bytes 6291464 | tf_op jit(solution)/shard_map/ppermute | solution.py:409
  115.9 77.7 %collective-permute-start.13 = (bf16[2,8,256,256]{3,2,1,0:T(8,128)(2,1)}, bf16[2,8,256,256]{3,2,1,0:T(8,128)(2,1)}, u32[]{:S(2)}, u32[]{:S(2)}) collective-permute-start(bf16[2,8,256,256]{3,2,1,0:T(8,128)(2,1)} %broadcast_select_fusion.3), channel_id=1, source_target_pairs={{0,2},{2,0},{1,3},{3,1},{4,6},{6,4},{5,7},{7,5},{8,10},{10,8},{9,1... | collective-permute-start | bytes 6291464 | tf_op jit(solution)/shard_map/ppermute | solution.py:412
  118.2 83.0 %collective-permute-start.22 = (bf16[2,8,256,256]{3,2,1,0:T(8,128)(2,1)}, bf16[2,8,256,256]{3,2,1,0:T(8,128)(2,1)}, u32[]{:S(2)}, u32[]{:S(2)}) collective-permute-start(bf16[2,8,256,256]{3,2,1,0:T(8,128)(2,1)} %get-tuple-element.49), channel_id=1, source_target_pairs={{0,4},{12,8},{1,5},{13,9},{2,6},{14,10},{3,7},{15,11},{16,20},{28,... | collective-permute-start | bytes 6291464 | tf_op jit(solution)/shard_map/ppermute | solution.py:410
  165.9 59.2 %collective-permute-start = (bf16[2,4,256,256]{3,2,1,0:T(8,128)(2,1)}, bf16[2,4,256,256]{3,2,1,0:T(8,128)(2,1)}, u32[]{:S(2)}, u32[]{:S(2)}) collective-permute-start(bf16[2,4,256,256]{3,2,1,0:T(8,128)(2,1)} %get-tuple-element.68), channel_id=1, source_target_pairs={{0,4},{12,8},{1,5},{13,9},{2,6},{14,10},{3,7},{15,11},{16,20},{28,... | collective-permute-start | bytes 3145736 | tf_op jit(solution)/shard_map/ppermute | solution.py:410
  168.2 58.9 %collective-permute-start.23 = (bf16[2,8,256,256]{3,2,1,0:T(8,128)(2,1)}, bf16[2,8,256,256]{3,2,1,0:T(8,128)(2,1)S(1)}, u32[]{:S(2)}, u32[]{:S(2)}) collective-permute-start(bf16[2,8,256,256]{3,2,1,0:T(8,128)(2,1)} %collective-permute-done.17.refs_1_), channel_id=1, source_target_pairs={{4,8},{8,4},{5,9},{9,5},{6,10},{10,6},{7,11},{11,7},{20,24},{24,20... | collective-permute-start | bytes 6291464 | tf_op jit(solution)/shard_map/ppermute | solution.py:411
  169.0 58.9 %collective-permute-start.21 = (bf16[2,8,256,256]{3,2,1,0:T(8,128)(2,1)}, bf16[2,8,256,256]{3,2,1,0:T(8,128)(2,1)S(1)}, u32[]{:S(2)}, u32[]{:S(2)}) collective-permute-start(bf16[2,8,256,256]{3,2,1,0:T(8,128)(2,1)} %collective-permute-done.15.refs_2_), channel_id=1, source_target_pairs={{4,0},{8,12},{5,1},{9,13},{6,2},{10,14},{7,3},{11,15},{20,16},{24,... | collective-permute-start | bytes 6291464 | tf_op jit(solution)/shard_map/ppermute | solution.py:409
  193.6 50.1 %collective-permute-start.19 = (bf16[2,2,2,2,512,128]{5,4,3,2,1,0:T(8,128)(2,1)}, bf16[2,2,2,2,512,128]{5,4,3,2,1,0:T(8,128)(2,1)}, u32[]{:S(2)}, u32[]{:S(2)}) collective-permute-start(bf16[2,2,2,2,512,128]{5,4,3,2,1,0:T(8,128)(2,1)} %pad_maximum_fusion), channel_id=1, source_target_pairs={{0,4},{12,8},{1,5},{13,9},{2,6},{14,10},{3,7},{15,11},{16,20},{28,... | collective-permute-start | bytes 6291464 | tf_op jit(solution)/shard_map/ppermute | solution.py:410
  201.2 46.1 %collective-permute-start.20 = (bf16[2,8,256,256]{3,2,1,0:T(8,128)(2,1)}, bf16[2,8,256,256]{3,2,1,0:T(8,128)(2,1)}, u32[]{:S(2)}, u32[]{:S(2)}) collective-permute-start(bf16[2,8,256,256]{3,2,1,0:T(8,128)(2,1)} %broadcast_select_fusion.2), channel_id=1, source_target_pairs={{0,2},{2,0},{1,3},{3,1},{4,6},{6,4},{5,7},{7,5},{8,10},{10,8},{9,1... | collective-permute-start | bytes 6291464 | tf_op jit(solution)/shard_map/ppermute | solution.py:412
  225.1 43.2 %collective-permute-start.24 = (bf16[2,8,256,256]{3,2,1,0:T(8,128)(2,1)}, bf16[2,8,256,256]{3,2,1,0:T(8,128)(2,1)}, u32[]{:S(2)}, u32[]{:S(2)}) collective-permute-start(bf16[2,8,256,256]{3,2,1,0:T(8,128)(2,1)} %collective-permute-done.22.refs_2_), channel_id=1, source_target_pairs={{4,8},{8,4},{5,9},{9,5},{6,10},{10,6},{7,11},{11,7},{20,24},{24,20... | collective-permute-start | bytes 6291464 | tf_op jit(solution)/shard_map/ppermute | solution.py:411
  227.1 55.0 %collective-permute-start.18 = (bf16[2,4,256,256]{3,2,1,0:T(8,128)(2,1)}, bf16[2,4,256,256]{3,2,1,0:T(8,128)(2,1)S(1)}, u32[]{:S(2)}, u32[]{:S(2)}) collective-permute-start(bf16[2,4,256,256]{3,2,1,0:T(8,128)(2,1)} %collective-permute-done.refs_0_), channel_id=1, source_target_pairs={{4,8},{8,4},{5,9},{9,5},{6,10},{10,6},{7,11},{11,7},{20,24},{24,20... | collective-permute-start | bytes 3145736 | tf_op jit(solution)/shard_map/ppermute | solution.py:411
  227.9 47.4 %collective-permute-start.25 = (bf16[2,8,256,256]{3,2,1,0:T(8,128)(2,1)S(1)}, bf16[2,8,256,256]{3,2,1,0:T(8,128)(2,1)S(1)}, u32[]{:S(2)}, u32[]{:S(2)}) collective-permute-start(bf16[2,8,256,256]{3,2,1,0:T(8,128)(2,1)S(1)} %collective-permute-done.23.refs_1_), channel_id=1, source_target_pairs={{4,0},{8,12},{5,1},{9,13},{6,2},{10,14},{7,3},{11,15},{20,16},{24,... | collective-permute-start | bytes 6291464 | tf_op jit(solution)/shard_map/ppermute | solution.py:409
  243.7 51.0 %collective-permute-start.29 = (bf16[2,2,2,2,512,128]{5,4,3,2,1,0:T(8,128)(2,1)}, bf16[2,2,2,2,512,128]{5,4,3,2,1,0:T(8,128)(2,1)}, u32[]{:S(2)}, u32[]{:S(2)}) collective-permute-start(bf16[2,2,2,2,512,128]{5,4,3,2,1,0:T(8,128)(2,1)} %collective-permute-done.19.t_ref), channel_id=1, source_target_pairs={{0,16},{16,0},{1,17},{17,1},{2,18},{18,2},{3,19},{19,3},{4,20},{20... | collective-permute-start | bytes 6291464 | tf_op jit(solution)/shard_map/ppermute | solution.py:414
  247.3 51.7 %collective-permute-start.28 = (bf16[2,8,256,256]{3,2,1,0:T(8,128)(2,1)}, bf16[2,8,256,256]{3,2,1,0:T(8,128)(2,1)}, u32[]{:S(2)}, u32[]{:S(2)}) collective-permute-start(bf16[2,8,256,256]{3,2,1,0:T(8,128)(2,1)} %broadcast_select_fusion.1), channel_id=1, source_target_pairs={{0,2},{2,0},{1,3},{3,1},{4,6},{6,4},{5,7},{7,5},{8,10},{10,8},{9,1... | collective-permute-start | bytes 6291464 | tf_op jit(solution)/shard_map/ppermute | solution.py:412
  268.3 52.5 %collective-permute-start.27 = (bf16[2,8,256,256]{3,2,1,0:T(8,128)(2,1)}, bf16[2,8,256,256]{3,2,1,0:T(8,128)(2,1)S(1)}, u32[]{:S(2)}, u32[]{:S(2)}) collective-permute-start(bf16[2,8,256,256]{3,2,1,0:T(8,128)(2,1)} %collective-permute-done.24.refs_4_), channel_id=1, source_target_pairs={{4,0},{8,12},{5,1},{9,13},{6,2},{10,14},{7,3},{11,15},{20,16},{24,... | collective-permute-start | bytes 6291464 | tf_op jit(solution)/shard_map/ppermute | solution.py:409
  277.3 63.8 %collective-permute-start.32 = (bf16[2,8,256,256]{3,2,1,0:T(8,128)(2,1)}, bf16[2,8,256,256]{3,2,1,0:T(8,128)(2,1)}, u32[]{:S(2)}, u32[]{:S(2)}) collective-permute-start(bf16[2,8,256,256]{3,2,1,0:T(8,128)(2,1)} %broadcast_select_fusion), channel_id=1, source_target_pairs={{0,2},{2,0},{1,3},{3,1},{4,6},{6,4},{5,7},{7,5},{8,10},{10,8},{9,1... | collective-permute-start | bytes 6291464 | tf_op jit(solution)/shard_map/ppermute | solution.py:412
  282.1 44.7 %collective-permute-start.31 = (bf16[2,4,256,256]{3,2,1,0:T(8,128)(2,1)S(1)}, bf16[2,4,256,256]{3,2,1,0:T(8,128)(2,1)S(1)}, u32[]{:S(2)}, u32[]{:S(2)}) collective-permute-start(bf16[2,4,256,256]{3,2,1,0:T(8,128)(2,1)S(1)} %copy-done.13), channel_id=1, source_target_pairs={{0,4},{12,8},{1,5},{13,9},{2,6},{14,10},{3,7},{15,11},{16,20},{28,... | collective-permute-start | bytes 3145736 | tf_op jit(solution)/shard_map/ppermute | solution.py:410
  323.9 36.7 %collective-permute-start.30 = (bf16[2,4,256,256]{3,2,1,0:T(8,128)(2,1)}, bf16[2,4,256,256]{3,2,1,0:T(8,128)(2,1)S(1)}, u32[]{:S(2)}, u32[]{:S(2)}) collective-permute-start(bf16[2,4,256,256]{3,2,1,0:T(8,128)(2,1)} %slice_select_fusion), channel_id=1, source_target_pairs={{0,2},{2,0},{1,3},{3,1},{4,6},{6,4},{5,7},{7,5},{8,10},{10,8},{9,1... | collective-permute-start | bytes 3145736 | tf_op jit(solution)/shard_map/ppermute | solution.py:412
  325.4 35.2 %collective-permute-start.26 = (bf16[2,4,256,256]{3,2,1,0:T(8,128)(2,1)S(1)}, bf16[2,4,256,256]{3,2,1,0:T(8,128)(2,1)S(1)}, u32[]{:S(2)}, u32[]{:S(2)}) collective-permute-start(bf16[2,4,256,256]{3,2,1,0:T(8,128)(2,1)S(1)} %collective-permute-done.18.refs_2_), channel_id=1, source_target_pairs={{4,0},{8,12},{5,1},{9,13},{6,2},{10,14},{7,3},{11,15},{20,16},{24,... | collective-permute-start | bytes 3145736 | tf_op jit(solution)/shard_map/ppermute | solution.py:409
  (25 other events, 352.0 us)
